TPU v7x, 32 devices: a whole 2x2x4 slice. The times are simulated.
32 devices in a mesh: batch: 16 (over z, y, core), tensor: 2 (over x).
Axes of the slice: x: 2, y: 2, z: 4, core: 2. Of those that a mesh axis runs over, the one named last changes fastest.
Arguments:
- activations: bfloat16 [65536, 768], P(('batch', 'tensor')), may hold values from -6 to 6
- cotangent: float32 [65536, 768], P(('batch', 'tensor')), may hold values from -6 to 6
- buckets: int32 [16], replicated, may hold values from 0 to 2, as said below
- lengths: int32 [16, 4], P('batch'), may hold values from 0 to 4096, as said below
- first_gain: bfloat16 [768], P(('batch', 'tensor')), may hold values from 0.5 to 1.5
- first_bias: bfloat16 [768], P(('batch', 'tensor')), may hold values from -2.5 to 2.5
- in_weight: bfloat16 [768, 2304], P(('batch', 'tensor')), may hold values from -0.21875 to 0.21875
- in_bias: bfloat16 [2304], P(('batch', 'tensor')), may hold values from -2.5 to 2.5
- short_kernel: bfloat16 [3, 768], P(None, ('batch', 'tensor')), may hold values from -3 to 3
- short_value: bfloat16 [3, 768], P(None, ('batch', 'tensor')), may hold values from -3 to 3
- out_weight: bfloat16 [768, 768], P(('batch', 'tensor')), may hold values from -0.3125 to 0.3125
- out_bias: bfloat16 [768], P(('batch', 'tensor')), may hold values from -2.5 to 2.5
- second_gain: bfloat16 [768], P(('batch', 'tensor')), may hold values from 0.5 to 1.5
- second_bias: bfloat16 [768], P(('batch', 'tensor')), may hold values from -2.5 to 2.5
- gate_weight: bfloat16 [768, 3072], P('batch', 'tensor'), may hold values from -0.21875 to 0.21875
- up_weight: bfloat16 [768, 3072], P('batch', 'tensor'), may hold values from -0.21875 to 0.21875
- down_weight: bfloat16 [3072, 768], P('tensor', 'batch'), may hold values from -0.15625 to 0.15625
Outputs:
- out_rows: float32 [65536, 768], P(('batch', 'tensor'))
- grad_activations: float32 [65536, 768], P(('batch', 'tensor'))
- grad_first_gain: float32 [768], P(('batch', 'tensor'))
- grad_first_bias: float32 [768], P(('batch', 'tensor'))
- grad_in_weight: float32 [768, 2304], P(('batch', 'tensor'))
- grad_in_bias: float32 [2304], P(('batch', 'tensor'))
- grad_short_kernel: float32 [3, 768], P(None, ('batch', 'tensor'))
- grad_short_value: float32 [3, 768], P(None, ('batch', 'tensor'))
- grad_out_weight: float32 [768, 768], P(('batch', 'tensor'))
- grad_out_bias: float32 [768], P(('batch', 'tensor'))
- grad_second_gain: float32 [768], P(('batch', 'tensor'))
- grad_second_bias: float32 [768], P(('batch', 'tensor'))
- grad_gate_weight: float32 [768, 3072], P('batch', 'tensor')
- grad_up_weight: float32 [768, 3072], P('batch', 'tensor')
- grad_down_weight: float32 [3072, 768], P('tensor', 'batch')
- norms: float32 [768], P(('batch', 'tensor'))
Inputs may be any that keep to these rules, and one draw needn't show every extreme that they name: The slots of batch index b are 4096 >> buckets[b] long. Batch index 0 always has bucket 0. Row b holds the lengths of the 2 ** buckets[b] sequences of batch index b in its first entries and 0 in the rest; each length is more than half of its slot and at most the slot. The first sequence of batch index 0 fills all 4096 slots.
All inputs are finite; a program needn't handle non-finite values.
Results may differ from a plain program's by a relative error of at most 0.015.
Values may be sent and summed in bfloat16 or wider, within the bound.
A program may use at most 1.0625 GiB of HBM per device.

v0:
```python
from functools import partial
import math

import jax
import jax.numpy as jnp
from jax import lax
from jax.sharding import PartitionSpec as P

EPS = 1e-05
TINY = 1e-06
HIGH = lax.Precision.HIGHEST


def norm_parts(values, gain, bias):
    row_mean = jnp.mean(values, -1, keepdims=True)
    centred = values - row_mean
    row_var = jnp.mean(centred * centred, -1, keepdims=True)
    inverse = lax.rsqrt(row_var + EPS)
    normed = centred * inverse
    return (normed * gain + bias, normed, inverse)


def norm_back(grad_out, normed, inverse, gain):
    scaled = grad_out * gain
    centre_term = jnp.mean(scaled, -1, keepdims=True)
    slope_term = jnp.mean(scaled * normed, -1, keepdims=True)
    return inverse * (scaled - centre_term - normed * slope_term)


def phase_table(row_count, col_count, period):
    product = (
        jnp.arange(row_count, dtype=jnp.int32)[:, None]
        * jnp.arange(col_count, dtype=jnp.int32)[None, :]
    )
    angles = (product % period).astype(jnp.float32) * (2.0 * math.pi / period)
    return (jnp.cos(angles), jnp.sin(angles))


def forward_transform(signal, tabs):
    cos_a, sin_a, cos_b, sin_b, twist_c, twist_s = tabs
    first_re = jnp.einsum("ka,msab->mskb", cos_a, signal, precision=HIGH)
    first_im = -jnp.einsum("ka,msab->mskb", sin_a, signal, precision=HIGH)
    turned_re = first_re * twist_c + first_im * twist_s
    turned_im = first_im * twist_c - first_re * twist_s
    spec_re = jnp.einsum("mskb,lb->mskl", turned_re, cos_b, precision=HIGH) + jnp.einsum(
        "mskb,lb->mskl", turned_im, sin_b, precision=HIGH
    )
    spec_im = jnp.einsum("mskb,lb->mskl", turned_im, cos_b, precision=HIGH) - jnp.einsum(
        "mskb,lb->mskl", turned_re, sin_b, precision=HIGH
    )
    return (spec_re, spec_im)


def inverse_transform(spec_re, spec_im, tabs):
    cos_a, sin_a, cos_b, sin_b, twist_c, twist_s = tabs
    back_re = jnp.einsum("mskl,lb->mskb", spec_re, cos_b, precision=HIGH) - jnp.einsum(
        "mskl,lb->mskb", spec_im, sin_b, precision=HIGH
    )
    back_im = jnp.einsum("mskl,lb->mskb", spec_im, cos_b, precision=HIGH) + jnp.einsum(
        "mskl,lb->mskb", spec_re, sin_b, precision=HIGH
    )
    turned_re = back_re * twist_c - back_im * twist_s
    turned_im = back_im * twist_c + back_re * twist_s
    return jnp.einsum("ka,mskb->msab", cos_a, turned_re, precision=HIGH) - jnp.einsum(
        "ka,mskb->msab", sin_a, turned_im, precision=HIGH
    )


def short_mix(slots, taps, slot_mask):
    one_back = jnp.pad(slots, ((0, 0), (0, 0), (1, 0)))[..., :-1]
    two_back = jnp.pad(slots, ((0, 0), (0, 0), (2, 0)))[..., :-2]
    return (
        taps[0][:, None, None] * slots
        + taps[1][:, None, None] * one_back
        + taps[2][:, None, None] * two_back
    ) * slot_mask


def slot_conv(slot_width, kernels, values, short_k, short_v, valid_rows):
    bin_rows = kernels.shape[0]
    channels = kernels.shape[1]
    slot_count = bin_rows // slot_width
    total = 2 * slot_width
    inner = min(128, total)
    outer = total // inner
    cos_a, sin_a = phase_table(outer, outer, outer)
    cos_b, sin_b = phase_table(inner, inner, inner)
    twist_c, twist_s = phase_table(outer, inner, total)
    tabs = (cos_a, sin_a, cos_b, sin_b, twist_c, twist_s)
    slot_mask = valid_rows[:, 0].reshape(1, slot_count, slot_width)
    kernel_short = short_mix(
        kernels.T.reshape(channels, slot_count, slot_width), short_k, slot_mask
    )
    value_short = short_mix(values.T.reshape(channels, slot_count, slot_width), short_v, slot_mask)
    kernel_norm = jnp.sqrt(jnp.sum(kernel_short * kernel_short, -1, keepdims=True) + TINY)
    kernel_unit = kernel_short / kernel_norm
    stacked = jnp.concatenate([kernel_unit, value_short], 0)
    padded = jnp.concatenate([stacked, jnp.zeros_like(stacked)], -1).reshape(
        2 * channels, slot_count, outer, inner
    )
    spec_re, spec_im = forward_transform(padded, tabs)
    power = spec_re[:channels] * spec_re[:channels] + spec_im[:channels] * spec_im[:channels]
    result = inverse_transform(power * spec_re[channels:], power * spec_im[channels:], tabs)
    result = result.reshape(channels, slot_count, total)[..., :slot_width] / total
    return (result.reshape(channels, bin_rows).T, jnp.sum(kernel_norm[..., 0], 1))


def on_device(
    activations,
    cotangent,
    buckets,
    lengths,
    first_gain,
    first_bias,
    in_weight,
    in_bias,
    short_kernel,
    short_value,
    out_weight,
    out_bias,
    second_gain,
    second_bias,
    gate_weight,
    up_weight,
    down_weight,
):
    width = activations.shape[1]
    f32 = jnp.float32
    bf16 = jnp.bfloat16
    params = (
        lax.all_gather(first_gain, ("batch", "tensor"), axis=0, tiled=True),
        lax.all_gather(first_bias, ("batch", "tensor"), axis=0, tiled=True),
        lax.all_gather(in_weight, ("batch", "tensor"), axis=0, tiled=True),
        lax.all_gather(in_bias, ("batch", "tensor"), axis=0, tiled=True),
        lax.all_gather(short_kernel, ("batch", "tensor"), axis=1, tiled=True),
        lax.all_gather(short_value, ("batch", "tensor"), axis=1, tiled=True),
        lax.all_gather(out_weight, ("batch", "tensor"), axis=0, tiled=True),
        lax.all_gather(out_bias, ("batch", "tensor"), axis=0, tiled=True),
        lax.all_gather(second_gain, ("batch", "tensor"), axis=0, tiled=True),
        lax.all_gather(second_bias, ("batch", "tensor"), axis=0, tiled=True),
    )
    gain_one = params[0].astype(f32)
    bias_one = params[1].astype(f32)
    in_full = params[2]
    in_shift = params[3].astype(f32)
    taps_kernel = params[4]
    taps_value = params[5]
    out_full = params[6]
    out_shift = params[7].astype(f32)
    gain_two = params[8].astype(f32)
    bias_two = params[9].astype(f32)
    shards = (
        lax.all_gather(gate_weight, "batch", axis=0, tiled=True),
        lax.all_gather(up_weight, "batch", axis=0, tiled=True),
        lax.all_gather(down_weight, "batch", axis=1, tiled=True),
    )
    rows_in = activations.astype(f32)
    first_out, first_hat, first_inv = norm_parts(rows_in, gain_one, bias_one)
    normed_first = first_out.astype(bf16)
    projected = jnp.dot(normed_first, in_full, preferred_element_type=f32) + in_shift
    queries = projected[:, :width]
    kernel_part, value_part = (
        lax.all_to_all(
            projected[:, width : 2 * width].astype(bf16),
            "tensor",
            split_axis=1,
            concat_axis=0,
            tiled=True,
        ),
        lax.all_to_all(
            projected[:, 2 * width :].astype(bf16),
            "tensor",
            split_axis=1,
            concat_axis=0,
            tiled=True,
        ),
    )
    bin_rows = kernel_part.shape[0]
    channels = kernel_part.shape[1]
    chan_start = lax.axis_index("tensor") * channels
    short_k = lax.dynamic_slice_in_dim(taps_kernel, chan_start, channels, 1).astype(f32)
    short_v = lax.dynamic_slice_in_dim(taps_value, chan_start, channels, 1).astype(f32)
    bucket_here = buckets[lax.axis_index("batch")]
    seq_lengths = lengths[0]
    position = jnp.arange(bin_rows, dtype=jnp.int32)
    slot_width = jnp.right_shift(jnp.int32(bin_rows), bucket_here)
    slot_index = position // slot_width
    within = position - slot_index * slot_width
    choose = slot_index[:, None] == jnp.arange(4, dtype=jnp.int32)[None, :]
    slot_limit = jnp.sum(jnp.where(choose, seq_lengths[None, :], 0), 1)
    valid_rows = (within < slot_limit).astype(f32)[:, None]
    kernels = kernel_part.astype(f32) * valid_rows
    values = value_part.astype(f32) * valid_rows
    branches = [partial(slot_conv, bin_rows >> bucket_level) for bucket_level in range(3)]

    def conv_apply(kernel_in, value_in, taps_k, taps_v):
        return lax.switch(bucket_here, branches, kernel_in, value_in, taps_k, taps_v, valid_rows)

    conv_out, conv_back, norm_part = jax.vjp(
        conv_apply, kernels, values, short_k, short_v, has_aux=True
    )
    mixed_rows = lax.all_to_all(
        (conv_out * valid_rows).astype(bf16), "tensor", split_axis=0, concat_axis=1, tiled=True
    )
    mixed = mixed_rows.astype(f32)
    gated = (queries * mixed).astype(bf16)
    middle = rows_in + jnp.dot(gated, out_full, preferred_element_type=f32) + out_shift
    second_out, second_hat, second_inv = norm_parts(middle, gain_two, bias_two)
    normed_second = second_out.astype(bf16)
    full_weights = (
        lax.all_gather(shards[0], "tensor", axis=1, tiled=True),
        lax.all_gather(shards[1], "tensor", axis=1, tiled=True),
        lax.all_gather(shards[2], "tensor", axis=0, tiled=True),
    )
    gate_pre = jnp.dot(normed_second, full_weights[0], preferred_element_type=f32)
    up_value = jnp.dot(normed_second, full_weights[1], preferred_element_type=f32)
    gate_sigmoid = jax.nn.sigmoid(gate_pre)
    gate_silu = gate_pre * gate_sigmoid
    hidden = (gate_silu * up_value).astype(bf16)
    out_rows = middle + jnp.dot(hidden, full_weights[2], preferred_element_type=f32)
    cot_low = cotangent.astype(bf16)
    d_hidden = jnp.einsum("rd,fd->rf", cot_low, full_weights[2], preferred_element_type=f32)
    down_whole = jnp.einsum("rf,rd->fd", hidden, cot_low, preferred_element_type=f32)
    d_up = (d_hidden * gate_silu).astype(bf16)
    d_gate = (d_hidden * up_value * gate_sigmoid * (1.0 + gate_pre * (1.0 - gate_sigmoid))).astype(
        bf16
    )
    gate_whole = jnp.einsum("rd,rf->df", normed_second, d_gate, preferred_element_type=f32)
    up_whole = jnp.einsum("rd,rf->df", normed_second, d_up, preferred_element_type=f32)
    d_second = jnp.einsum(
        "rf,df->rd", d_gate, full_weights[0], preferred_element_type=f32
    ) + jnp.einsum("rf,df->rd", d_up, full_weights[1], preferred_element_type=f32)
    grad_gate, grad_up, grad_down = (
        lax.psum_scatter(
            gate_whole.astype(jnp.bfloat16), "tensor", scatter_dimension=1, tiled=True
        ).astype(jnp.float32),
        lax.psum_scatter(
            up_whole.astype(jnp.bfloat16), "tensor", scatter_dimension=1, tiled=True
        ).astype(jnp.float32),
        lax.psum_scatter(
            down_whole.astype(jnp.bfloat16), "tensor", scatter_dimension=0, tiled=True
        ).astype(jnp.float32),
    )
    mlp_summed = (
        lax.psum_scatter(
            grad_gate.astype(jnp.bfloat16), "batch", scatter_dimension=0, tiled=True
        ).astype(jnp.float32),
        lax.psum_scatter(
            grad_up.astype(jnp.bfloat16), "batch", scatter_dimension=0, tiled=True
        ).astype(jnp.float32),
        lax.psum_scatter(
            grad_down.astype(jnp.bfloat16), "batch", scatter_dimension=1, tiled=True
        ).astype(jnp.float32),
    )
    grad_middle = cotangent + norm_back(d_second, second_hat, second_inv, gain_two)
    grad_gain_two = jnp.sum(d_second * second_hat, 0)
    grad_bias_two = jnp.sum(d_second, 0)
    d_mix = grad_middle.astype(bf16)
    grad_out_full = jnp.einsum("rd,re->de", gated, d_mix, preferred_element_type=f32)
    grad_out_shift = jnp.sum(d_mix.astype(f32), 0)
    d_gated = jnp.einsum("re,de->rd", d_mix, out_full, preferred_element_type=f32)
    d_queries = d_gated * mixed
    d_mixed = (d_gated * queries).astype(bf16)
    d_mixed_chan = lax.all_to_all(d_mixed, "tensor", split_axis=1, concat_axis=0, tiled=True)
    d_kernels_f, d_values_f, d_taps_k, d_taps_v = conv_back(d_mixed_chan.astype(f32) * valid_rows)
    d_kernel_rows, d_value_rows = (
        lax.all_to_all(
            (d_kernels_f * valid_rows).astype(bf16),
            "tensor",
            split_axis=0,
            concat_axis=1,
            tiled=True,
        ),
        lax.all_to_all(
            (d_values_f * valid_rows).astype(bf16),
            "tensor",
            split_axis=0,
            concat_axis=1,
            tiled=True,
        ),
    )
    d_projected = jnp.concatenate([d_queries.astype(bf16), d_kernel_rows, d_value_rows], 1)
    grad_in_full = jnp.einsum("rd,rk->dk", normed_first, d_projected, preferred_element_type=f32)
    grad_in_shift = jnp.sum(d_projected.astype(f32), 0)
    d_first = jnp.einsum("rk,dk->rd", d_projected, in_full, preferred_element_type=f32)
    grad_activations = grad_middle + norm_back(d_first, first_hat, first_inv, gain_one)
    grad_gain_one = jnp.sum(d_first * first_hat, 0)
    grad_bias_one = jnp.sum(d_first, 0)
    taps_zero = jnp.zeros((3, width), f32)
    taps_k_full = lax.dynamic_update_slice(taps_zero, d_taps_k, (jnp.int32(0), chan_start))
    taps_v_full = lax.dynamic_update_slice(taps_zero, d_taps_v, (jnp.int32(0), chan_start))
    norm_full = lax.dynamic_update_slice(jnp.zeros((width,), f32), norm_part, (chan_start,))
    summed = (
        lax.psum_scatter(grad_gain_one, ("batch", "tensor"), scatter_dimension=0, tiled=True),
        lax.psum_scatter(grad_bias_one, ("batch", "tensor"), scatter_dimension=0, tiled=True),
        lax.psum_scatter(grad_in_full, ("batch", "tensor"), scatter_dimension=0, tiled=True),
        lax.psum_scatter(grad_in_shift, ("batch", "tensor"), scatter_dimension=0, tiled=True),
        lax.psum_scatter(taps_k_full, ("batch", "tensor"), scatter_dimension=1, tiled=True),
        lax.psum_scatter(taps_v_full, ("batch", "tensor"), scatter_dimension=1, tiled=True),
        lax.psum_scatter(grad_out_full, ("batch", "tensor"), scatter_dimension=0, tiled=True),
        lax.psum_scatter(grad_out_shift, ("batch", "tensor"), scatter_dimension=0, tiled=True),
        lax.psum_scatter(grad_gain_two, ("batch", "tensor"), scatter_dimension=0, tiled=True),
        lax.psum_scatter(grad_bias_two, ("batch", "tensor"), scatter_dimension=0, tiled=True),
        lax.psum_scatter(norm_full, ("batch", "tensor"), scatter_dimension=0, tiled=True),
    )
    seq_count = jnp.sum(jnp.left_shift(jnp.ones_like(buckets), buckets)).astype(f32)
    return (
        out_rows,
        grad_activations,
        summed[0],
        summed[1],
        summed[2],
        summed[3],
        summed[4],
        summed[5],
        summed[6],
        summed[7],
        summed[8],
        summed[9],
        mlp_summed[0],
        mlp_summed[1],
        mlp_summed[2],
        summed[10] / seq_count,
    )


def solution(mesh):
    return jax.shard_map(
        on_device,
        mesh=mesh,
        in_specs=(
            P(("batch", "tensor"), None),
            P(("batch", "tensor"), None),
            P(),
            P("batch", None),
            P(("batch", "tensor")),
            P(("batch", "tensor")),
            P(("batch", "tensor"), None),
            P(("batch", "tensor")),
            P(None, ("batch", "tensor")),
            P(None, ("batch", "tensor")),
            P(("batch", "tensor"), None),
            P(("batch", "tensor")),
            P(("batch", "tensor")),
            P(("batch", "tensor")),
            P("batch", "tensor"),
            P("batch", "tensor"),
            P("tensor", "batch"),
        ),
        out_specs=(
            P(("batch", "tensor"), None),
            P(("batch", "tensor"), None),
            P(("batch", "tensor")),
            P(("batch", "tensor")),
            P(("batch", "tensor"), None),
            P(("batch", "tensor")),
            P(None, ("batch", "tensor")),
            P(None, ("batch", "tensor")),
            P(("batch", "tensor"), None),
            P(("batch", "tensor")),
            P(("batch", "tensor")),
            P(("batch", "tensor")),
            P("batch", "tensor"),
            P("batch", "tensor"),
            P("tensor", "batch"),
            P(("batch", "tensor")),
        ),
        check_vma=False,
    )
```

profile of v0, /device:TPU:0, one launch (start us, length us, event | category | flops | bytes accessed | tf_op | source)
XLA Modules:
  0.0 2508.3 jit_solution(6107673846244335319)
XLA Ops:
  15.7 42.4 %all-reduce.82 = (bf16[2304]{0:T(1024)(128)(2,1)S(1)}, bf16[768]{0:T(1024)(128)(2,1)S(1)}, bf16[768]{0:T(1024)(128)(2,1)S(1)}, bf16[768]{0:T(1024)(128)(2,1)}, b...) all-reduce(bf16[2304]{0:T(1024)(128)(2,1)S(1)} %dynamic-update-slic, ...), channel_id=1, replica_groups=mesh['batch'=16,'tensor'=2] {'batch','tensor'}, use_global_device_ids=true, to_apply=%add.68 | all-reduce | flops 6144 | bytes 24576
  62.8 54.7 %all-gather.11.cloned.1.call-done = bf16[768,2304]{1,0:T(8,128)(2,1)} async-done(((bf16[24,2304]{1,0:T(8,128)(2,1)}), bf16[768,2304]{1,0:T(8,128)(2,1)}) %all-gather.11.cloned.1.call-update) | async-done | bytes 3538960 | tf_op jit(solution)/shard_map/all_gather | solution.py:133
  143.2 32.9 %all-to-all-done = bf16[2048,2,384]{2,0,1:T(8,128)(2,1)S(1)} async-done(((bf16[2048,2,384]{2,0,1:T(8,128)(2,1)}), bf16[2048,2,384]{2,0,1:T(8,128)(2,1)S(1)}, u32[]{:S(2)}, u32[]{:S(2)}) %all-to-all-start) | async-done | bytes 3145760 | tf_op jit(solution)/shard_map/all_to_all | solution.py:163
  181.4 93.3 %all-gather = bf16[32,24,3]{1,2,0:T(4,128)(2,1)S(1)} all-gather(bf16[1,24,3]{1,2,0:T(4,128)(2,1)S(1)} %bitcast.844), channel_id=1, replica_groups=mesh['batch'=16,'tensor'=2] {'batch','tensor'}, dimensions={0}, use_global_device_ids=true | all-gather | bytes 4752 | tf_op jit(solution)/shard_map/all_gather | solution.py:135
  274.9 65.0 %all-gather.1 = bf16[32,24,3]{1,2,0:T(4,128)(2,1)S(1)} all-gather(bf16[1,24,3]{1,2,0:T(4,128)(2,1)S(1)} %bitcast.845), channel_id=1, replica_groups=mesh['batch'=16,'tensor'=2] {'batch','tensor'}, dimensions={0}, use_global_device_ids=true | all-gather | bytes 4752 | tf_op jit(solution)/shard_map/all_gather | solution.py:136
  382.3 661.9 %conditional.2 = (f32[4096,384]{0,1:T(8,128)}, f32[384]{0:T(512)}, f32[384,1,4096]{2,0,1:T(8,128)}, f32[384,1,1]{0,2,1:T(1,128)}, f32[384,1,4096]{2,0,1:T(8,128)...) conditional(s32[]{:T(128)} %bitcast.193, ...), branch_computations={%region_3.5_spmd, %region_5.8_spmd, %region_8.11_spmd} | conditional | flops 72635375616 | bytes 1493120896 | solution.py:197
  383.0 32.1 %multiply_reduce_fusion = (f32[384]{0:T(512)S(1)}, f32[384,1,4096]{2,0,1:T(8,128)}, f32[384,1,4096]{2,0,1:T(8,128)}, f32[384,1,4096]{2,0,1:T(8,128)}, f32[384,1,...) fusion(f32[4096]{0:T(1024)S(1)} %get-tuple-element.455, f32[384]{0:T(512)S(1)} %get-tuple-element.2185, ...), kind=kLoop, calls=%fused_computation.47 | loop fusion | flops 22019712 | bytes 62941696 | tf_op jit(solution)/shard_map/jvp()/cond/branch_0_fun/reduce_sum | solution.py:95
  438.3 30.0 %fusion.58 = f32[768,128,64]{1,2,0:T(8,128)} fusion(f32[768,64,128]{2,1,0:T(8,128)} %bitcast.770, f32[64,64]{0,1:T(8,128)S(1)} %get-tuple-element.2360), kind=kOutput, calls=%fused_computation.91 | convolution fusion | flops 4831838208 | bytes 50348032 | tf_op jit(solution)/shard_map/jvp()/cond/branch_0_fun/ka,msab->mskb/dot_general | solution.py:42
  468.5 42.0 %fusion.2 = (f32[768,64,128]{2,1,0:T(8,128)}, f32[768,64,128]{2,1,0:T(8,128)}) fusion(f32[768,128,64]{1,2,0:T(8,128)} %fusion.58, f32[64,128]{1,0:T(8,128)S(1)} %get-tuple-element.2190, f32[64,128]{1,0:T(8,128)S(1)} %get-tuple-element.2191, f32[768,64,128]{2,1,0:T(8,128)} %bitcast.771, f32[64,64]{0,1:T(8,128)S(1)} %get-tuple-element.2359), kind=kOutput, calls=%fused_computation.6 | convolution fusion | flops 4875878400 | bytes 100745216 | tf_op jit(solution)/shard_map/jvp()/cond/branch_0_fun/ka,msab->mskb/dot_general | solution.py:41
  510.8 44.7 %fusion.7 = f32[768,64,128]{2,0,1:T(8,128)} fusion(f32[768,64,128]{2,1,0:T(8,128)} %get-tuple-element.2161, f32[128,128]{1,0:T(8,128)S(1)} %get-tuple-element.2364), kind=kOutput, calls=%fused_computation.13 | convolution fusion | flops 9663676416 | bytes 50397184 | tf_op jit(solution)/shard_map/jvp()/cond/branch_0_fun/mskb,lb->mskl/dot_general | solution.py:45
  555.6 44.0 %fusion.22 = f32[768,64,128]{2,0,1:T(8,128)} fusion(f32[768,64,128]{2,0,1:T(8,128)} %fusion.7, f32[768,64,128]{2,1,0:T(8,128)S(1)} %bitcast.769, f32[128,128]{1,0:T(8,128)S(1)} %get-tuple-element.2363), kind=kOutput, calls=%fused_computation.48 | convolution fusion | flops 9669967872 | bytes 75563008 | tf_op jit(solution)/shard_map/jvp()/cond/branch_0_fun/mskb,lb->mskl/dot_general | solution.py:45
  599.6 43.9 %fusion.5 = f32[768,64,128]{2,0,1:T(8,128)} fusion(f32[768,64,128]{2,1,0:T(8,128)} %get-tuple-element.2161, f32[128,128]{1,0:T(8,128)S(1)} %get-tuple-element.2363), kind=kOutput, calls=%fused_computation.11 | convolution fusion | flops 9663676416 | bytes 50397184 | tf_op jit(solution)/shard_map/jvp()/cond/branch_0_fun/mskb,lb->mskl/dot_general | solution.py:48
  643.5 44.0 %fusion.25 = f32[768,64,128]{2,0,1:T(8,128)} fusion(f32[768,64,128]{2,0,1:T(8,128)} %fusion.5, f32[768,64,128]{2,1,0:T(8,128)S(1)} %bitcast.769, f32[128,128]{1,0:T(8,128)S(1)} %get-tuple-element.2364), kind=kOutput, calls=%fused_computation.49 | convolution fusion | flops 9669967872 | bytes 75563008 | tf_op jit(solution)/shard_map/jvp()/cond/branch_0_fun/mskb,lb->mskl/dot_general | solution.py:48
  687.6 37.2 %slice_bitcast_fusion = (f32[384,1,64,128]{3,0,2,1:T(8,128)}, f32[384,1,64,128]{3,0,2,1:T(8,128)}, f32[384,64,128]{2,0,1:T(8,128)}, f32[384,1,64,128]{3,0,2,1:T(8,128)}, f32[384,1,64,128]{3,0,2,1:T(8,128)}) fusion(f32[768,64,128]{2,0,1:T(8,128)} %fusion.25, f32[768,64,128]{2,0,1:T(8,128)} %fusion.22), kind=kLoop, calls=%fused_computation.27 | loop fusion | flops 9437184 | bytes 113246208 | tf_op jit(solution)/shard_map/jvp()/cond/branch_0_fun/slice | solution.py:103
  744.0 28.9 %fusion.29 = f32[384,64,128]{2,0,1:T(8,128)} fusion(f32[384,64,128]{2,0,1:T(8,128)} %get-tuple-element.2164, f32[768,64,128]{2,0,1:T(8,128)} %fusion.22, f32[128,128]{1,0:T(8,128)S(1)} %get-tuple-element.2363), kind=kOutput, calls=%fused_computation.51 | convolution fusion | flops 4834983936 | bytes 37814272 | tf_op jit(solution)/shard_map/jvp()/cond/branch_0_fun/mskl,lb->mskb/dot_general | solution.py:56
  788.0 30.3 %multiply_subtract_fusion = (f32[384,64,128]{2,0,1:T(8,128)}, f32[384,64,128]{2,0,1:T(8,128)}) fusion(f32[64,128]{1,0:T(8,128)S(1)} %copy-done.48, f32[64,128]{1,0:T(8,128)S(1)} %copy-done.50, f32[384,64,128]{2,0,1:T(8,128)} %fusion.28, f32[384,64,128]{2,0,1:T(8,128)} %fusion.29, f32[384,64,128]{2,0,1:T(8,128)} %fusion.31, ...), kind=kOutput, calls=%fused_computation.25 | convolution fusion | flops 4860149760 | bytes 88211456 | tf_op jit(solution)/shard_map/jvp()/cond/branch_0_fun/mskl,lb->mskb/dot_general | solution.py:59
  840.7 28.2 %subtract_bitcast_fusion = f32[384,1,64,128]{3,2,0,1:T(8,128)} fusion(f32[384,128,64]{1,2,0:T(8,128)S(1)} %fusion.13, f32[384,64,128]{2,0,1:T(8,128)} %get-tuple-element.2158, f32[64,64]{0,1:T(8,128)S(1)} %copy-done.32), kind=kOutput, calls=%fused_computation.23 | convolution fusion | flops 2419064832 | bytes 37765120 | tf_op jit(solution)/shard_map/jvp()/cond/branch_0_fun/ka,mskb->msab/dot_general | solution.py:64
  1132.7 130.2 %all-gather.25.cloned.1.call-done = bf16[3072,768]{0,1:T(8,128)(2,1)} async-done(((bf16[1536,768]{0,1:T(8,128)(2,1)}), bf16[3072,768]{0,1:T(8,128)(2,1)}) %all-gather.25.cloned.1.call-update) | async-done | bytes 4718608 | tf_op jit(solution)/shard_map/all_gather | solution.py:213
  1262.9 38.7 %multiply_convert_fusion = (bf16[2048,3072]{1,0:T(8,128)(2,1)}, bf16[2048,3072]{1,0:T(8,128)(2,1)}, bf16[2048,3072]{1,0:T(8,128)(2,1)}) fusion(f32[2048,3072]{1,0:T(8,128)} %fusion.463, f32[2048,3072]{1,0:T(8,128)} %fusion.464, bf16[3072,768]{0,1:T(8,128)(2,1)} %all-gather.25.cloned.1.call-done, f32[2048,768]{1,0:T(8,128)} %param.24), kind=kOutput, calls=%fused_computation.641 | convolution fusion | flops 9759621120 | bytes 99090432 | tf_op jit(solution)/shard_map/rd,fd->rf/dot_general | solution.py:222
  1370.4 32.5 %reduce-scatter.25.cloned.1.call-done = bf16[1536,768]{1,0:T(8,128)(2,1)} async-done(((bf16[3072,768]{1,0:T(8,128)(2,1)}), bf16[1536,768]{1,0:T(8,128)(2,1)}) %reduce-scatter.25.cloned.1.call-update) | async-done | bytes 2359312 | tf_op jit(solution)/shard_map/reduce_scatter | solution.py:240
  1435.4 29.7 %reduce-scatter.21.cloned.1.call-done = bf16[768,1536]{1,0:T(8,128)(2,1)} async-done(((bf16[768,3072]{1,0:T(8,128)(2,1)}), bf16[768,1536]{1,0:T(8,128)(2,1)}) %reduce-scatter.21.cloned.1.call-update) | async-done | bytes 2359312 | tf_op jit(solution)/shard_map/reduce_scatter | solution.py:237
  1476.7 73.4 %all_to_all.90 = bf16[2048,2,384]{2,0,1:T(8,128)(2,1)S(1)} all-to-all(bf16[2048,2,384]{2,0,1:T(8,128)(2,1)S(1)} %bitcast.817), channel_id=1, replica_groups=mesh['batch'=16,'tensor'=2] {'tensor'}, dimensions={1} | all-to-all | bytes 6291456 | tf_op jit(solution)/shard_map/all_to_all | solution.py:264
  1563.7 556.5 %conditional.3 = (f32[4096,384]{0,1:T(8,128)}, f32[4096,384]{0,1:T(8,128)}, f32[3,384]{1,0:T(4,128)S(1)}, f32[3,384]{1,0:T(4,128)S(1)}) conditional(s32[]{:T(128)} %bitcast.193, (f32[384,1,1]{0,2,1:T(1,128)}, f32[4096,384]{0,1:T(8,128)S(1)}, f32[64,64]{0,1:T(8,128)S(1)}, f32[1,1,64,128]{3,2,1,0:T(8,128)S(1)}, ...), branch_computations={%region_15.23_spmd, %region_23.31_spmd, %region_31.39_spmd} | conditional | flops 72711938048 | bytes 1227680000 | solution.py:197
  1600.1 27.7 %negate_bitcast_fusion.1 = (f32[384,64,128]{2,1,0:T(8,128)}, f32[384,64,128]{2,1,0:T(8,128)}, f32[384,64,128]{2,1,0:T(8,128)}) fusion(f32[64,128]{1,0:T(8,128)S(1)} %bitcast.828, f32[64,128]{1,0:T(8,128)S(1)} %bitcast.826, f32[384,128,64]{1,2,0:T(8,128)} %fusion.260, f32[64,64]{0,1:T(8,128)S(1)} %get-tuple-element.473, f32[384,1,64,128]{3,2,0,1:T(8,128)} %bitcast.779), kind=kOutput, calls=%fused_computation.409 | convolution fusion | flops 2441084928 | bytes 62996480 | tf_op jit(solution)/shard_map/transpose(jvp())/cond/branch_0_fun/ka,mskb->msab/dot_general | solution.py:64
  1695.4 49.1 %fusion.441 = (f32[384,1,64,128]{3,0,2,1:T(8,128)}, f32[384,1,64,128]{3,0,2,1:T(8,128)}, f32[384,1,64,128]{3,0,2,1:T(8,128)}, f32[384,1,64,128]{3,0,2,1:T(8,128)}) fusion(f32[384,1,64,128]{3,0,2,1:T(8,128)} %get-tuple-element.480, f32[384,1,64,128]{3,0,2,1:T(8,128)} %get-tuple-element.479, f32[384,64,128]{2,0,1:T(8,128)} %fusion.267, ...), kind=kOutput, calls=%fused_computation.727 | convolution fusion | flops 4857004032 | bytes 151060480 | tf_op jit(solution)/shard_map/transpose(jvp())/cond/branch_0_fun/mskl,lb->mskb/dot_general | solution.py:59
  1744.5 26.3 %fusion.256 = f32[768,64,128]{2,0,1:T(8,128)} fusion(f32[384,1,64,128]{3,0,2,1:T(8,128)} %get-tuple-element.2144, f32[384,1,64,128]{3,0,2,1:T(8,128)} %get-tuple-element.2290, f32[128,128]{1,0:T(8,128)S(1)} %get-tuple-element.476), kind=kOutput, calls=%fused_computation.387 | convolution fusion | flops 9676259328 | bytes 50397184 | tf_op jit(solution)/shard_map/transpose(jvp())/cond/branch_0_fun/mskb,lb->mskl/dot_general | solution.py:45
  1861.4 49.7 %negate_bitcast_fusion = (f32[768,128,64]{1,0,2:T(8,128)}, f32[768,128,64]{1,0,2:T(8,128)}) fusion(f32[64,128]{1,0:T(8,128)S(1)} %bitcast.827, f32[64,128]{1,0:T(8,128)S(1)} %bitcast.829, f32[768,64,128]{2,0,1:T(8,128)} %fusion.245, f32[768,64,128]{2,0,1:T(8,128)} %fusion.254, f32[768,64,128]{2,0,1:T(8,128)} %fusion.247, f32[768,64,128]{2,0,1:T(8,128)} %fusion.256), kind=kLoop, calls=%fused_computation.384 | loop fusion | flops 62914560 | bytes 151060480 | tf_op jit(solution)/shard_map/reshape.136
  1911.0 46.8 %fusion.249 = f32[768,128,64]{1,2,0:T(8,128)} fusion(f32[768,128,64]{1,0,2:T(8,128)} %get-tuple-element.2283, f32[64,64]{0,1:T(8,128)S(1)} %copy-done.36), kind=kOutput, calls=%fused_computation.378 | convolution fusion | flops 4831838208 | bytes 50348032 | tf_op jit(solution)/shard_map/transpose(jvp())/cond/branch_0_fun/ka,msab->mskb/dot_general | solution.py:41
  1957.9 52.0 %add_bitcast_fusion = f32[768,1,64,128]{3,2,0,1:T(8,128)} fusion(f32[768,128,64]{1,2,0:T(8,128)} %fusion.249, f32[768,128,64]{1,0,2:T(8,128)} %get-tuple-element.2282, f32[64,64]{0,1:T(8,128)S(1)} %copy-done.42), kind=kOutput, calls=%fused_computation.382 | convolution fusion | flops 4838129664 | bytes 75513856 | tf_op jit(solution)/shard_map/transpose(jvp())/cond/branch_0_fun/ka,msab->mskb/dot_general | solution.py:42
  2009.9 27.5 %reshape.939 = f32[768,1,8192]{2,0,1:T(8,128)} reshape(f32[768,1,64,128]{3,2,0,1:T(8,128)} %add_bitcast_fusion) | data formatting | bytes 50331648 | tf_op jit(solution)/shard_map/transpose(jvp())/cond/branch_0_fun/reshape | solution.py:98
  2256.4 146.4 %all-reduce.81 = (f32[768]{0:T(1024)S(1)}, f32[768]{0:T(1024)S(1)}, f32[2304]{0:T(1024)S(1)}, f32[3,768]{1,0:T(4,128)S(1)}, f32[3,768]{1,0:T(4,128)S(1)}, /*inde...) all-reduce(f32[768]{0:T(1024)S(1)} %get-tuple-element.2102, ...), channel_id=2, replica_groups=mesh['batch'=16,'tensor'=2] {'batch','tensor'}, use_global_device_ids=true, to_apply=%region_42.43.clone | all-reduce | flops 11520 | bytes 92160
  2428.2 73.3 %reduce-scatter.13.cloned.1.call-done = f32[24,2304]{1,0:T(8,128)} async-done(((f32[768,2304]{1,0:T(8,128)}), f32[24,2304]{1,0:T(8,128)}) %reduce-scatter.13.cloned.1.call-update) | async-done | bytes 221200 | tf_op jit(solution)/shard_map/reduce_scatter | solution.py:296
  (473 shorter events, 966.4 us)
Async XLA Ops:
  7.2 55.6 %all-gather.15.cloned.1.call-start = ((), (), s32[]{:S(2)}) async-start(), calls=%async_computation.16 | async-start | bytes 2506752 | tf_op jit(solution)/shard_map/all_gather | solution.py:153
  7.9 109.5 %all-gather.11.cloned.1.call-start = ((), (), s32[]{:S(2)}) async-start(), calls=%async_computation.14 | async-start | bytes 3649536 | tf_op jit(solution)/shard_map/all_gather | solution.py:133
  8.7 331.3 %all-gather.19.cloned.1.call-start = ((), (), s32[]{:S(2)}) async-start(), calls=%async_computation.18 | async-start | bytes 2506752 | tf_op jit(solution)/shard_map/all_gather | solution.py:154
  9.4 1052.4 %all-gather.23.cloned.1.call-start = ((), (), s32[]{:S(2)}) async-start(), calls=%async_computation.20 | async-start | bytes 2506752 | tf_op jit(solution)/shard_map/all_gather | solution.py:155
  10.0 1081.3 %all-gather.13.cloned.1.call-start = ((), (), s32[]{:S(2)}) async-start(), calls=%async_computation.15 | async-start | bytes 1216512 | tf_op jit(solution)/shard_map/all_gather | solution.py:137
  10.6 1090.5 %all-gather.17.cloned.1.call-start = ((), (), s32[]{:S(2)}) async-start(), calls=%async_computation.17 | async-start | bytes 7077888 | tf_op jit(solution)/shard_map/all_gather | solution.py:211
  58.1 73.2 %copy-start.93 = (f32[768]{0:T(1024)}, f32[768]{0:T(1024)S(1)}, u32[]{:S(2)}) copy-start(f32[768]{0:T(1024)S(1)} %convert_element_type.379) | copy-start | bytes 9220
  58.1 73.2 %copy-start.115 = (f32[768]{0:T(1024)}, f32[768]{0:T(1024)S(1)}, u32[]{:S(2)}) copy-start(f32[768]{0:T(1024)S(1)} %convert_element_type.380) | copy-start | bytes 9220
  61.3 70.0 %copy-start.2 = (bf16[2048,768]{0,1:T(8,128)(2,1)}, bf16[2048,768]{0,1:T(8,128)(2,1)S(1)}, u32[]{:S(2)}) copy-start(bf16[2048,768]{0,1:T(8,128)(2,1)S(1)} %copy.675) | copy-start | bytes 9437188
  61.8 69.5 %copy-start.83 = (f32[2048]{0:T(1024)}, f32[2048]{0:T(1024)S(1)}, u32[]{:S(2)}) copy-start(f32[2048]{0:T(1024)S(1)} %broadcast_multiply_fusion.20) | copy-start | bytes 24580
  62.7 68.6 %copy-start.87 = (f32[2048]{0:T(1024)}, f32[2048]{0:T(1024)S(1)}, u32[]{:S(2)}) copy-start(f32[2048]{0:T(1024)S(1)} %add_rsqrt_fusion.1) | copy-start | bytes 24580
  133.4 141.5 %copy-start.123 = (bf16[3,24]{1,0:T(4,128)(2,1)S(1)}, bf16[3,24]{1,0:T(4,128)(2,1)}, u32[]{:S(2)}) copy-start(bf16[3,24]{1,0:T(4,128)(2,1)} %param.32) | copy-start | bytes 436
  133.4 206.6 %copy-start.125 = (s32[16]{0:T(128)S(1)}, s32[16]{0:T(128)}, u32[]{:S(2)}) copy-start(s32[16]{0:T(128)} %param.25) | copy-start | bytes 196
  133.4 208.7 %copy-start.124 = (s32[1,4]{1,0:T(1,128)S(1)}, s32[1,4]{1,0:T(1,128)}, u32[]{:S(2)}) copy-start(s32[1,4]{1,0:T(1,128)} %param.26) | copy-start | bytes 52
  135.4 40.7 %all-to-all-start = ((bf16[2048,2,384]{2,0,1:T(8,128)(2,1)}), bf16[2048,2,384]{2,0,1:T(8,128)(2,1)S(1)}, u32[]{:S(2)}, u32[]{:S(2)}) async-start(bf16[2048,2,384]{2,0,1:T(8,128)(2,1)} %bitcast.761), calls=%async_computation | async-start | bytes 6291456 | tf_op jit(solution)/shard_map/all_to_all | solution.py:163
  176.1 176.8 %all-to-all-start.1 = ((bf16[2048,2,384]{2,0,1:T(8,128)(2,1)}), bf16[2048,2,384]{2,0,1:T(8,128)(2,1)}, u32[]{:S(2)}, u32[]{:S(2)}) async-start(bf16[2048,2,384]{2,0,1:T(8,128)(2,1)} %bitcast.760), calls=%async_computation.1 | async-start | bytes 6291456 | tf_op jit(solution)/shard_map/all_to_all | solution.py:170
  181.4 935.7 %all-gather.21.cloned.1.call-start = ((), (), s32[]{:S(2)}) async-start(), calls=%async_computation.19 | async-start | bytes 7077888 | tf_op jit(solution)/shard_map/all_gather | solution.py:212
  510.7 262.1 %copy-start.11 = (f32[128,128]{1,0:T(8,128)}, f32[128,128]{1,0:T(8,128)S(1)}, u32[]{:S(2)}) copy-start(f32[128,128]{1,0:T(8,128)S(1)} %get-tuple-element.2364) | copy-start | bytes 196612 | tf_op jit(solution)/shard_map/jvp()/cond
  510.8 277.2 %copy-start.15 = (f32[128,128]{1,0:T(8,128)}, f32[128,128]{1,0:T(8,128)S(1)}, u32[]{:S(2)}) copy-start(f32[128,128]{1,0:T(8,128)S(1)} %get-tuple-element.2363) | copy-start | bytes 196612 | tf_op jit(solution)/shard_map/jvp()/cond
  1057.7 24.6 all-to-all-start.2
  1061.7 201.3 %all-gather.25.cloned.1.call-start = ((), (), s32[]{:S(2)}) async-start(), calls=%async_computation.21 | async-start | bytes 7077888 | tf_op jit(solution)/shard_map/all_gather | solution.py:213
  1062.4 340.5 %reduce-scatter.25.cloned.1.call-start = ((), (), s32[]{:S(2)}) async-start(), calls=%async_computation.28 | async-start | bytes 7077888 | tf_op jit(solution)/shard_map/reduce_scatter | solution.py:240
  1318.2 146.9 %reduce-scatter.21.cloned.1.call-start = ((), (), s32[]{:S(2)}) async-start(), calls=%async_computation.26 | async-start | bytes 7077888 | tf_op jit(solution)/shard_map/reduce_scatter | solution.py:237
  1332.6 787.6 %reduce-scatter.17.cloned.1.call-start = ((), (), s32[]{:S(2)}) async-start(), calls=%async_computation.24 | async-start | bytes 7077888 | tf_op jit(solution)/shard_map/reduce_scatter | solution.py:234
  1347.1 1075.8 %reduce-scatter.27.cloned.1.call-start = ((), (), s32[]{:S(2)}) async-start(), calls=%async_computation.29 | async-start | bytes 2506752
  1407.2 1017.7 %reduce-scatter.23.cloned.1.call-start = ((), (), s32[]{:S(2)}) async-start(), calls=%async_computation.27 | async-start | bytes 2506752 | tf_op jit(solution)/shard_map/reduce_scatter | solution.py:248
  1465.2 961.4 %reduce-scatter.19.cloned.1.call-start = ((), (), s32[]{:S(2)}) async-start(), calls=%async_computation.25 | async-start | bytes 2506752 | tf_op jit(solution)/shard_map/reduce_scatter | solution.py:245
  1563.7 557.1 %copy-start.23 = (f32[4096]{0:T(1024)S(1)}, f32[4096]{0:T(1024)}, u32[]{:S(2)}) copy-start(f32[4096]{0:T(1024)} %copy-done.21) | copy-start | bytes 49156
  2131.5 24.6 all-to-all-start.4
  2157.8 26.0 %all-to-all-start.5 = ((bf16[2,2048,384]{2,1,0:T(8,128)(2,1)}), bf16[2,2048,384]{2,1,0:T(8,128)(2,1)}, u32[]{:S(2)}, u32[]{:S(2)}) async-start(bf16[2,2048,384]{2,1,0:T(8,128)(2,1)} %bitcast.815), calls=%async_computation.5 | async-start | bytes 6291456 | tf_op jit(solution)/shard_map/all_to_all | solution.py:274
  2163.1 265.2 %reduce-scatter.15.cloned.1.call-start = ((), (), s32[]{:S(2)}) async-start(), calls=%async_computation.23 | async-start | bytes 2433024 | tf_op jit(solution)/shard_map/reduce_scatter | solution.py:300
  2171.1 330.5 %reduce-scatter.13.cloned.1.call-start = ((), (), s32[]{:S(2)}) async-start(), calls=%async_computation.22 | async-start | bytes 7299072 | tf_op jit(solution)/shard_map/reduce_scatter | solution.py:296
  (98 other events, 2068.5 us)
Sparse Core Ops, SparseCore 0:
  10.3 45.2 all-gather.14
  58.5 58.9 all-gather.10
  119.7 40.9 all-gather.18
  162.9 41.0 all-gather.22
  206.8 52.9 all-gather.12
  261.1 62.1 all-gather.16
  340.1 59.3 all-gather.20
  1064.1 198.8 all-gather.24
  1318.4 84.5 reduce-scatter.24
  1405.2 59.9 reduce-scatter.20
  1467.5 93.7 reduce-scatter.16
  1565.3 62.9 reduce-scatter.26
  1632.1 61.9 reduce-scatter.22
  2120.4 151.9 reduce-scatter.18
  2278.2 98.0 reduce-scatter.14
  2383.3 118.2 reduce-scatter.12
where the time goes:
time: 2520 us; the launch traced here: 2510 us
  matrix products  989 us (39%)
  blocking collectives  420 us (17%)
  waiting for transfers between devices  402 us (16%)
  local copies, waits for them, and re-layouts  332 us (13%)
  other arithmetic  297 us (12%)
  loops' own time  28 us (1%)
    unnamed x2, blocking collectives  189 us
    another operation x40, local copies, waits for them, and re-layouts  142 us
    all_gather x1, waiting for transfers between devices, on_device(): lax.all_gather(shards[2], 'tensor', axis=0, tiled=True)  130 us
    all_gather x1, blocking collectives, on_device(): lax.all_gather(short_kernel, ('batch', 'tensor'), axis=1, tiled=True)  93.3 us
    dot_general x2, matrix products, forward_transform(): first_re = jnp.einsum('ka,msab->mskb', cos_a, signal, precision=HIGH)  88.8 us
    dot_general x2, matrix products, forward_transform(): first_im = -jnp.einsum('ka,msab->mskb', sin_a, signal, precision=HIGH)  82 us
    all_to_all x1, blocking collectives, on_device(): lax.all_to_all(d_mixed, 'tensor', split_axis=1, concat_axis=0, tiled=True)  73.4 us
    reduce_scatter x1, waiting for transfers between devices, on_device(): lax.psum_scatter(grad_in_full, ('batch', 'tensor'), scatter_dimension=0,...  73.3 us
  transfers between devices with their start and end apart: 21, of which 9 were waited for; matrix products, arithmetic and copies ran while one was open for 62% of the time, Pallas kernels for 0%

commit v1 on v0

v1 whole, which is shorter than its diff:
```python
import math

import jax
import jax.numpy as jnp
import numpy as np
from jax import lax
from jax.experimental import pallas as pl
from jax.experimental.pallas import tpu as pltpu
from jax.sharding import PartitionSpec as P

EPS = 1e-05
TINY = 1e-06
LANES = 128
INNER = 128
OCTET = 8
f32 = jnp.float32
bf16 = jnp.bfloat16


def first_stage(outer, level):
    part = outer >> level
    index = np.arange(part)
    angle = (index[:, None] + 0.5) * index[None, :] * (math.pi / part)
    block = np.stack([np.cos(angle), -np.sin(angle)], 1).reshape(2 * part, part)
    return np.kron(np.eye(1 << level), block)


def turn_table(outer, level):
    part = outer >> level
    index = np.arange(outer) % part
    angle = (index[:, None] + 0.5) * np.arange(INNER)[None, :] * (math.pi / (part * INNER))
    return np.stack([np.cos(angle), np.sin(angle)])


def conv_tables(bin_rows, bucket, limits):
    outer = bin_rows // INNER
    levels = range(3)
    eye = np.eye(OCTET)
    firsts = [first_stage(outer, n) for n in levels]
    ones = np.stack([np.kron(item, eye) for item in firsts])
    backs = np.stack([np.kron(firsts[n].T / (bin_rows >> n), eye) for n in levels])
    turns = np.stack([turn_table(outer, n) for n in levels])
    inner_angle = (np.arange(INNER)[:, None] * np.arange(INNER)[None, :] % INNER) * (
        2.0 * math.pi / INNER
    )
    stage_one = jnp.asarray(ones, bf16)[bucket]
    back_one = jnp.asarray(backs, bf16)[bucket]
    turn = jnp.asarray(turns, f32)[bucket]
    base_c = jnp.asarray(np.cos(inner_angle), f32)
    base_s = jnp.asarray(np.sin(inner_angle), f32)
    cos_l = base_c[None] * turn[0][:, None, :] - base_s[None] * turn[1][:, None, :]
    sin_l = base_s[None] * turn[0][:, None, :] + base_c[None] * turn[1][:, None, :]
    stage_two = jnp.concatenate(
        [jnp.concatenate([cos_l, sin_l], 2), jnp.concatenate([-sin_l, cos_l], 2)], 1
    ).astype(bf16)
    cos_t = base_c[None] * turn[0][:, :, None] - base_s[None] * turn[1][:, :, None]
    sin_t = base_s[None] * turn[0][:, :, None] + base_c[None] * turn[1][:, :, None]
    back_two = jnp.concatenate(
        [jnp.concatenate([cos_t, -sin_t], 2), jnp.concatenate([sin_t, cos_t], 2)], 1
    ).astype(bf16)
    part = jnp.right_shift(jnp.int32(outer), bucket)
    chunk = jnp.arange(outer, dtype=jnp.int32)
    slot = chunk // part
    within = chunk - slot * part
    limit = jnp.sum(
        jnp.where(slot[:, None] == jnp.arange(limits.shape[0])[None, :], limits[None, :], 0), 1
    )
    room = jnp.broadcast_to((limit - within * INNER)[:, None], (outer, LANES)).astype(jnp.int32)
    joined = jnp.concatenate([(within > 0).astype(f32), jnp.zeros((OCTET,), f32)])
    joined = jnp.broadcast_to(joined[:, None], (outer + OCTET, LANES))
    same = (slot[:, None] == slot[None, :]).astype(f32)
    return (stage_one, stage_two, back_two, back_one, room, joined, same)


def shifted_back(now, before, iota):
    one = jnp.where(iota == 0, before[15:16], pltpu.roll(now, 1, 0))
    two = jnp.where(
        iota == 0, before[14:15], jnp.where(iota == 1, before[15:16], pltpu.roll(now, 2, 0))
    )
    return (one, two)


def load_chunk(ref, chunk, joined_row):
    now = ref[pl.ds(pl.multiple_of(chunk * INNER, INNER), INNER), :].astype(f32)
    at = pl.multiple_of(jnp.maximum(chunk * INNER - 16, 0), 16)
    before = ref[pl.ds(at, 16), :].astype(f32) * joined_row
    return (now, before)


def conv_forward_kernel(
    kern_ref, val_ref, taps_k, taps_v, one_ref, two_ref, back_two_ref, back_one_ref,
    room_ref, joined_ref, same_ref,
    out_ref, unit_ref, vspec_ref, norm_ref,
    time_buf, mid_buf, low_buf, square_buf,
):
    outer = kern_ref.shape[0] // INNER
    iota = lax.broadcasted_iota(jnp.int32, (INNER, LANES), 0)

    def prepare(chunk, carry):
        joined = joined_ref[pl.ds(chunk, 1), :]
        valid = iota < room_ref[pl.ds(chunk, 1), :]
        now, before = load_chunk(kern_ref, chunk, joined)
        one, two = shifted_back(now, before, iota)
        kern = jnp.where(valid, taps_k[0:1] * now + taps_k[1:2] * one + taps_k[2:3] * two, 0.0)
        time_buf[chunk, :, 0:LANES] = kern
        square_buf[pl.ds(chunk, 1), :] = jnp.sum(kern * kern, 0, keepdims=True)
        now, before = load_chunk(val_ref, chunk, joined)
        one, two = shifted_back(now, before, iota)
        val = jnp.where(valid, taps_v[0:1] * now + taps_v[1:2] * one + taps_v[2:3] * two, 0.0)
        time_buf[chunk, :, LANES:] = val
        return carry

    lax.fori_loop(0, outer, prepare, 0)
    total = jnp.dot(same_ref[...], square_buf[...], precision=lax.Precision.HIGHEST)
    norm = jnp.sqrt(total + TINY)
    norm_ref[...] = norm
    square_buf[...] = 1.0 / norm

    def stage_one(pair, carry):
        at = pl.multiple_of(pair * 16, 16)
        halves = []
        for half in range(2):
            part = time_buf[:, pl.ds(at + half * OCTET, OCTET), :]
            part = part.reshape(outer * OCTET, 2 * LANES).astype(bf16)
            done = jnp.dot(one_ref[...], part, preferred_element_type=f32)
            halves.append(done.reshape(2 * outer, OCTET, 2 * LANES))
        mid_buf[:, pl.ds(at, 16), :] = jnp.concatenate(halves, 1).astype(bf16)
        return carry

    lax.fori_loop(0, INNER // 16, stage_one, 0)

    def stage_two(kk, carry):
        row = pl.multiple_of(kk * 2, 2)
        part = mid_buf[pl.ds(row, 2)].reshape(2 * INNER, 2 * LANES)
        spec = jnp.dot(two_ref[kk], part, preferred_element_type=f32)
        inverse = square_buf[pl.ds(kk, 1), :]
        unit_re = spec[:INNER, :LANES] * inverse
        unit_im = spec[INNER:, :LANES] * inverse
        val_re = spec[:INNER, LANES:]
        val_im = spec[INNER:, LANES:]
        unit_ref[row] = unit_re.astype(bf16)
        unit_ref[row + 1] = unit_im.astype(bf16)
        vspec_ref[row] = val_re.astype(bf16)
        vspec_ref[row + 1] = val_im.astype(bf16)
        power = unit_re * unit_re + unit_im * unit_im
        made = jnp.concatenate([power * val_re, power * val_im], 0).astype(bf16)
        back = jnp.dot(back_two_ref[kk], made, preferred_element_type=f32)
        low_buf[row] = back[:INNER]
        low_buf[row + 1] = back[INNER:]
        return carry

    lax.fori_loop(0, outer, stage_two, 0, unroll=2)
    spot = lax.broadcasted_iota(jnp.int32, (outer, 16, LANES), 1)

    def back_one(pair, carry):
        at = pl.multiple_of(pair * 16, 16)
        halves = []
        for half in range(2):
            part = low_buf[:, pl.ds(at + half * OCTET, OCTET), :]
            part = part.reshape(2 * outer * OCTET, LANES).astype(bf16)
            done = jnp.dot(back_one_ref[...], part, preferred_element_type=f32)
            halves.append(done.reshape(outer, OCTET, LANES))
        whole = jnp.concatenate(halves, 1)
        valid = spot + at < room_ref[...][:, None, :]
        out_ref[:, pl.ds(at, 16), :] = jnp.where(valid, whole, 0.0).astype(bf16)
        return carry

    lax.fori_loop(0, INNER // 16, back_one, 0)


def conv_backward_kernel(
    grad_ref, kern_ref, val_ref, unit_ref, vspec_ref, norm_ref, taps_k, taps_v,
    one_ref, two_ref, back_two_ref, back_one_ref, room_ref, joined_ref, same_ref,
    dkern_ref, dval_ref, dtaps_k, dtaps_v,
    time_buf, mid_buf, low_buf, dots_buf, inv_buf,
):
    outer = kern_ref.shape[0] // INNER
    iota = lax.broadcasted_iota(jnp.int32, (INNER, LANES), 0)
    spot = lax.broadcasted_iota(jnp.int32, (outer, 16, LANES), 1)

    def stage_one(pair, carry):
        at = pl.multiple_of(pair * 16, 16)
        whole = grad_ref[:, pl.ds(at, 16), :].astype(f32)
        whole = jnp.where(spot + at < room_ref[...][:, None, :], whole, 0.0)
        halves = []
        for half in range(2):
            part = whole[:, half * OCTET : (half + 1) * OCTET]
            part = part.reshape(outer * OCTET, LANES).astype(bf16)
            done = jnp.dot(one_ref[...], part, preferred_element_type=f32)
            halves.append(done.reshape(2 * outer, OCTET, LANES))
        mid_buf[:, pl.ds(at, 16), :] = jnp.concatenate(halves, 1).astype(bf16)
        return carry

    lax.fori_loop(0, INNER // 16, stage_one, 0)

    def stage_two(kk, carry):
        row = pl.multiple_of(kk * 2, 2)
        part = mid_buf[pl.ds(row, 2)].reshape(2 * INNER, LANES)
        spec = jnp.dot(two_ref[kk], part, preferred_element_type=f32)
        grad_re = spec[:INNER]
        grad_im = spec[INNER:]
        unit_re = unit_ref[row].astype(f32)
        unit_im = unit_ref[row + 1].astype(f32)
        val_re = vspec_ref[row].astype(f32)
        val_im = vspec_ref[row + 1].astype(f32)
        power = unit_re * unit_re + unit_im * unit_im
        slope = 2.0 * (grad_re * val_re + grad_im * val_im)
        dots_buf[pl.ds(kk, 1), :] = jnp.sum(power * slope, 0, keepdims=True)
        upper = jnp.concatenate([power * grad_re, slope * unit_re], 1)
        lower = jnp.concatenate([power * grad_im, slope * unit_im], 1)
        made = jnp.concatenate([upper, lower], 0).astype(bf16)
        back = jnp.dot(back_two_ref[kk], made, preferred_element_type=f32)
        low_buf[row] = back[:INNER]
        low_buf[row + 1] = back[INNER:]
        return carry

    lax.fori_loop(0, outer, stage_two, 0, unroll=2)

    def back_one(octet, carry):
        at = pl.multiple_of(octet * OCTET, OCTET)
        part = low_buf[:, pl.ds(at, OCTET), :]
        part = part.reshape(2 * outer * OCTET, 2 * LANES).astype(bf16)
        done = jnp.dot(back_one_ref[...], part, preferred_element_type=f32)
        time_buf[:, pl.ds(at, OCTET), :] = done.reshape(outer, OCTET, 2 * LANES)
        return carry

    lax.fori_loop(0, INNER // OCTET, back_one, 0)
    inv_buf[...] = 1.0 / norm_ref[...]
    same = same_ref[...]
    share = same / (jnp.sum(same, 1, keepdims=True) * INNER)
    dots_buf[...] = jnp.dot(share, dots_buf[...], precision=lax.Precision.HIGHEST)

    def shifted_ahead(now, after):
        one = jnp.where(iota == INNER - 1, after[0:1], pltpu.roll(now, INNER - 1, 0))
        two = jnp.where(
            iota == INNER - 1,
            after[1:2],
            jnp.where(iota == INNER - 2, after[0:1], pltpu.roll(now, INNER - 2, 0)),
        )
        return (one, two)

    def finish(step, carry):
        after_k, after_v, sums = carry
        chunk = outer - 1 - step
        joined = joined_ref[pl.ds(chunk, 1), :]
        ahead = joined_ref[pl.ds(chunk + 1, 1), :]
        valid = iota < room_ref[pl.ds(chunk, 1), :]
        inverse = inv_buf[pl.ds(chunk, 1), :]
        along = dots_buf[pl.ds(chunk, 1), :]
        rows = pl.ds(pl.multiple_of(chunk * INNER, INNER), INNER)
        now, before = load_chunk(kern_ref, chunk, joined)
        one, two = shifted_back(now, before, iota)
        unit = (taps_k[0:1] * now + taps_k[1:2] * one + taps_k[2:3] * two) * inverse
        grad = jnp.where(valid, (time_buf[chunk, :, LANES:] - unit * along) * inverse, 0.0)
        ahead_one, ahead_two = shifted_ahead(grad, after_k * ahead)
        dkern_ref[rows, :] = (
            taps_k[0:1] * grad + taps_k[1:2] * ahead_one + taps_k[2:3] * ahead_two
        ).astype(bf16)
        made = [jnp.sum(grad * item, 0, keepdims=True) for item in (now, one, two)]
        after_k = grad[:OCTET]
        now, before = load_chunk(val_ref, chunk, joined)
        one, two = shifted_back(now, before, iota)
        grad = jnp.where(valid, time_buf[chunk, :, :LANES], 0.0)
        ahead_one, ahead_two = shifted_ahead(grad, after_v * ahead)
        dval_ref[rows, :] = (
            taps_v[0:1] * grad + taps_v[1:2] * ahead_one + taps_v[2:3] * ahead_two
        ).astype(bf16)
        made += [jnp.sum(grad * item, 0, keepdims=True) for item in (now, one, two)]
        after_v = grad[:OCTET]
        return (after_k, after_v, tuple(a + b for a, b in zip(sums, made)))

    zero = jnp.zeros((OCTET, LANES), f32)
    start = (zero, zero, tuple(jnp.zeros((1, LANES), f32) for _ in range(6)))
    _, _, sums = lax.fori_loop(0, outer, finish, start)
    for index in range(3):
        dtaps_k[index : index + 1, :] = sums[index]
        dtaps_v[index : index + 1, :] = sums[3 + index]


def whole_spec(shape):
    return pl.BlockSpec(shape, lambda c: (0,) * len(shape), pipeline_mode=pl.Buffered(1))


def lane_spec(rows):
    return pl.BlockSpec((rows, LANES), lambda c: (0, c))


def cube_spec(depth, rows):
    return pl.BlockSpec((depth, rows, LANES), lambda c: (0, 0, c))


def conv_forward(kern, val, taps_k, taps_v, tables):
    bin_rows, channels = kern.shape
    outer = bin_rows // INNER
    out, unit, vspec, norm = pl.pallas_call(
        conv_forward_kernel,
        grid=(channels // LANES,),
        in_specs=[lane_spec(bin_rows), lane_spec(bin_rows), lane_spec(3), lane_spec(3)]
        + [whole_spec(item.shape) for item in tables],
        out_specs=[
            cube_spec(outer, INNER),
            cube_spec(2 * outer, INNER),
            cube_spec(2 * outer, INNER),
            lane_spec(outer),
        ],
        out_shape=[
            jax.ShapeDtypeStruct((outer, INNER, channels), bf16),
            jax.ShapeDtypeStruct((2 * outer, INNER, channels), bf16),
            jax.ShapeDtypeStruct((2 * outer, INNER, channels), bf16),
            jax.ShapeDtypeStruct((outer, channels), f32),
        ],
        scratch_shapes=[
            pltpu.VMEM((outer, INNER, 2 * LANES), f32),
            pltpu.VMEM((2 * outer, INNER, 2 * LANES), bf16),
            pltpu.VMEM((2 * outer, INNER, LANES), f32),
            pltpu.VMEM((outer, LANES), f32),
        ],
        compiler_params=pltpu.CompilerParams(vmem_limit_bytes=56 << 20),
        cost_estimate=pl.CostEstimate(
            flops=26 * channels * bin_rows * 512, bytes_accessed=30 * bin_rows * channels, transcendentals=0
        ),
        name="conv_forward",
    )(kern, val, taps_k, taps_v, *tables)
    return (out.reshape(bin_rows, channels), unit, vspec, norm)


def conv_backward(grad, kern, val, unit, vspec, norm, taps_k, taps_v, tables):
    bin_rows, channels = kern.shape
    outer = bin_rows // INNER
    return pl.pallas_call(
        conv_backward_kernel,
        grid=(channels // LANES,),
        in_specs=[
            cube_spec(outer, INNER), lane_spec(bin_rows), lane_spec(bin_rows),
            cube_spec(2 * outer, INNER), cube_spec(2 * outer, INNER), lane_spec(outer),
            lane_spec(3), lane_spec(3),
        ]
        + [whole_spec(item.shape) for item in tables],
        out_specs=[lane_spec(bin_rows), lane_spec(bin_rows), lane_spec(3), lane_spec(3)],
        out_shape=[
            jax.ShapeDtypeStruct((bin_rows, channels), bf16),
            jax.ShapeDtypeStruct((bin_rows, channels), bf16),
            jax.ShapeDtypeStruct((3, channels), f32),
            jax.ShapeDtypeStruct((3, channels), f32),
        ],
        scratch_shapes=[
            pltpu.VMEM((outer, INNER, 2 * LANES), f32),
            pltpu.VMEM((2 * outer, INNER, LANES), bf16),
            pltpu.VMEM((2 * outer, INNER, 2 * LANES), f32),
            pltpu.VMEM((outer, LANES), f32),
            pltpu.VMEM((outer, LANES), f32),
        ],
        compiler_params=pltpu.CompilerParams(vmem_limit_bytes=56 << 20),
        cost_estimate=pl.CostEstimate(
            flops=30 * channels * bin_rows * 512, bytes_accessed=40 * bin_rows * channels, transcendentals=0
        ),
        name="conv_backward",
    )(grad.reshape(outer, INNER, channels), kern, val, unit, vspec, norm, taps_k, taps_v, *tables)


def norm_parts(values, gain, bias):
    row_mean = jnp.mean(values, -1, keepdims=True)
    centred = values - row_mean
    row_var = jnp.mean(centred * centred, -1, keepdims=True)
    inverse = lax.rsqrt(row_var + EPS)
    normed = centred * inverse
    return (normed * gain + bias, normed, inverse)


def norm_back(grad_out, normed, inverse, gain):
    scaled = grad_out * gain
    centre_term = jnp.mean(scaled, -1, keepdims=True)
    slope_term = jnp.mean(scaled * normed, -1, keepdims=True)
    return inverse * (scaled - centre_term - normed * slope_term)


def pad_lanes(array):
    extra = -array.shape[-1] % LANES
    if extra == 0:
        return array
    return jnp.pad(array, ((0, 0),) * (array.ndim - 1) + ((0, extra),))


def on_device(
    activations,
    cotangent,
    buckets,
    lengths,
    first_gain,
    first_bias,
    in_weight,
    in_bias,
    short_kernel,
    short_value,
    out_weight,
    out_bias,
    second_gain,
    second_bias,
    gate_weight,
    up_weight,
    down_weight,
):
    width = activations.shape[1]
    both = ("batch", "tensor")
    shard_rows = in_weight.shape[0]
    small = jnp.concatenate(
        [
            first_gain[:, None],
            first_bias[:, None],
            out_bias[:, None],
            second_gain[:, None],
            second_bias[:, None],
            short_kernel.T,
            short_value.T,
            in_bias.reshape(shard_rows, 3),
        ],
        1,
    )
    mixer = lax.all_gather(
        jnp.concatenate([in_weight, out_weight, pad_lanes(small)], 1), both, axis=0, tiled=True
    )
    in_full = mixer[:, : 3 * width]
    out_full = mixer[:, 3 * width : 4 * width]
    rows_small = mixer[:, 4 * width : 4 * width + 14].astype(f32).T
    gain_one, bias_one, out_shift, gain_two, bias_two = (rows_small[n] for n in range(5))
    taps_kernel = rows_small[5:8]
    taps_value = rows_small[8:11]
    in_shift = rows_small[11:14].T.reshape(3 * width)
    shards = (
        lax.all_gather(gate_weight, "batch", axis=0, tiled=True),
        lax.all_gather(up_weight, "batch", axis=0, tiled=True),
        lax.all_gather(down_weight, "batch", axis=1, tiled=True),
    )
    rows_in = activations.astype(f32)
    first_out, first_hat, first_inv = norm_parts(rows_in, gain_one, bias_one)
    normed_first = first_out.astype(bf16)
    projected = jnp.dot(normed_first, in_full, preferred_element_type=f32) + in_shift
    queries = projected[:, :width]
    kernels, values = (
        lax.all_to_all(
            projected[:, n * width : (n + 1) * width].astype(bf16),
            "tensor",
            split_axis=1,
            concat_axis=0,
            tiled=True,
        )
        for n in (1, 2)
    )
    bin_rows, channels = kernels.shape
    chan_start = lax.axis_index("tensor") * channels
    short_k = pad_lanes(lax.dynamic_slice_in_dim(taps_kernel, chan_start, channels, 1))
    short_v = pad_lanes(lax.dynamic_slice_in_dim(taps_value, chan_start, channels, 1))
    kernels = pad_lanes(kernels)
    values = pad_lanes(values)
    bucket_here = buckets[lax.axis_index("batch")]
    tables = conv_tables(bin_rows, bucket_here, lengths[0])
    mixed_chan, unit_spec, value_spec, norms = conv_forward(
        kernels, values, short_k, short_v, tables
    )
    norm_part = jnp.sum(norms[:, :channels], 0) / (bin_rows // INNER) * jnp.left_shift(
        jnp.int32(1), bucket_here
    ).astype(f32)
    mixed = lax.all_to_all(
        mixed_chan[:, :channels], "tensor", split_axis=0, concat_axis=1, tiled=True
    ).astype(f32)
    gated = (queries * mixed).astype(bf16)
    middle = rows_in + jnp.dot(gated, out_full, preferred_element_type=f32) + out_shift
    second_out, second_hat, second_inv = norm_parts(middle, gain_two, bias_two)
    normed_second = second_out.astype(bf16)
    full_weights = (
        lax.all_gather(shards[0], "tensor", axis=1, tiled=True),
        lax.all_gather(shards[1], "tensor", axis=1, tiled=True),
        lax.all_gather(shards[2], "tensor", axis=0, tiled=True),
    )
    gate_pre = jnp.dot(normed_second, full_weights[0], preferred_element_type=f32)
    up_value = jnp.dot(normed_second, full_weights[1], preferred_element_type=f32)
    gate_sigmoid = jax.nn.sigmoid(gate_pre)
    gate_silu = gate_pre * gate_sigmoid
    hidden = (gate_silu * up_value).astype(bf16)
    out_rows = middle + jnp.dot(hidden, full_weights[2], preferred_element_type=f32)
    cot_low = cotangent.astype(bf16)
    d_hidden = jnp.einsum("rd,fd->rf", cot_low, full_weights[2], preferred_element_type=f32)
    down_whole = jnp.einsum("rf,rd->fd", hidden, cot_low, preferred_element_type=f32)
    d_up = (d_hidden * gate_silu).astype(bf16)
    d_gate = (d_hidden * up_value * gate_sigmoid * (1.0 + gate_pre * (1.0 - gate_sigmoid))).astype(
        bf16
    )
    gate_whole = jnp.einsum("rd,rf->df", normed_second, d_gate, preferred_element_type=f32)
    up_whole = jnp.einsum("rd,rf->df", normed_second, d_up, preferred_element_type=f32)
    d_second = jnp.einsum(
        "rf,df->rd", d_gate, full_weights[0], preferred_element_type=f32
    ) + jnp.einsum("rf,df->rd", d_up, full_weights[1], preferred_element_type=f32)
    mlp_summed = tuple(
        lax.psum_scatter(
            lax.psum_scatter(
                grad.astype(bf16), "tensor", scatter_dimension=1 - dim, tiled=True
            ),
            "batch",
            scatter_dimension=dim,
            tiled=True,
        ).astype(f32)
        for grad, dim in ((gate_whole, 0), (up_whole, 0), (down_whole, 1))
    )
    grad_middle = cotangent + norm_back(d_second, second_hat, second_inv, gain_two)
    grad_gain_two = jnp.sum(d_second * second_hat, 0)
    grad_bias_two = jnp.sum(d_second, 0)
    d_mix = grad_middle.astype(bf16)
    grad_out_full = jnp.einsum("rd,re->de", gated, d_mix, preferred_element_type=f32)
    grad_out_shift = jnp.sum(d_mix.astype(f32), 0)
    d_gated = jnp.einsum("re,de->rd", d_mix, out_full, preferred_element_type=f32)
    d_queries = d_gated * mixed
    d_mixed = (d_gated * queries).astype(bf16)
    d_mixed_chan = lax.all_to_all(d_mixed, "tensor", split_axis=1, concat_axis=0, tiled=True)
    d_kernels, d_values, d_taps_k, d_taps_v = conv_backward(
        pad_lanes(d_mixed_chan), kernels, values, unit_spec, value_spec, norms,
        short_k, short_v, tables,
    )
    d_kernel_rows, d_value_rows = (
        lax.all_to_all(item[:, :channels], "tensor", split_axis=0, concat_axis=1, tiled=True)
        for item in (d_kernels, d_values)
    )
    d_projected = jnp.concatenate([d_queries.astype(bf16), d_kernel_rows, d_value_rows], 1)
    grad_in_full = jnp.einsum("rd,rk->dk", normed_first, d_projected, preferred_element_type=f32)
    grad_in_shift = jnp.sum(d_projected.astype(f32), 0)
    d_first = jnp.einsum("rk,dk->rd", d_projected, in_full, preferred_element_type=f32)
    grad_activations = grad_middle + norm_back(d_first, first_hat, first_inv, gain_one)
    grad_gain_one = jnp.sum(d_first * first_hat, 0)
    grad_bias_one = jnp.sum(d_first, 0)
    chan_rows = jnp.concatenate(
        [d_taps_k[:, :channels], d_taps_v[:, :channels], norm_part[None]], 0
    )
    chan_full = lax.dynamic_update_slice(
        jnp.zeros((7, width), f32), chan_rows, (jnp.int32(0), chan_start)
    )
    small_rows = jnp.concatenate(
        [
            grad_gain_one[None],
            grad_bias_one[None],
            grad_out_shift[None],
            grad_gain_two[None],
            grad_bias_two[None],
            chan_full,
            grad_in_shift.reshape(width, 3).T,
        ],
        0,
    )
    small_sum = lax.psum_scatter(
        pad_lanes(small_rows.T), both, scatter_dimension=0, tiled=True
    )
    mixer_sum = lax.psum_scatter(
        jnp.concatenate([grad_in_full.astype(bf16), grad_out_full.astype(bf16)], 1),
        both,
        scatter_dimension=0,
        tiled=True,
    ).astype(f32)
    seq_count = jnp.sum(jnp.left_shift(jnp.ones_like(buckets), buckets)).astype(f32)
    return (
        out_rows,
        grad_activations,
        small_sum[:, 0],
        small_sum[:, 1],
        mixer_sum[:, : 3 * width],
        small_sum[:, 12:15].reshape(3 * shard_rows),
        small_sum[:, 5:8].T,
        small_sum[:, 8:11].T,
        mixer_sum[:, 3 * width :],
        small_sum[:, 2],
        small_sum[:, 3],
        small_sum[:, 4],
        mlp_summed[0],
        mlp_summed[1],
        mlp_summed[2],
        small_sum[:, 11] / seq_count,
    )


def solution(mesh):
    return jax.shard_map(
        on_device,
        mesh=mesh,
        in_specs=(
            P(("batch", "tensor"), None),
            P(("batch", "tensor"), None),
            P(),
            P("batch", None),
            P(("batch", "tensor")),
            P(("batch", "tensor")),
            P(("batch", "tensor"), None),
            P(("batch", "tensor")),
            P(None, ("batch", "tensor")),
            P(None, ("batch", "tensor")),
            P(("batch", "tensor"), None),
            P(("batch", "tensor")),
            P(("batch", "tensor")),
            P(("batch", "tensor")),
            P("batch", "tensor"),
            P("batch", "tensor"),
            P("tensor", "batch"),
        ),
        out_specs=(
            P(("batch", "tensor"), None),
            P(("batch", "tensor"), None),
            P(("batch", "tensor")),
            P(("batch", "tensor")),
            P(("batch", "tensor"), None),
            P(("batch", "tensor")),
            P(None, ("batch", "tensor")),
            P(None, ("batch", "tensor")),
            P(("batch", "tensor"), None),
            P(("batch", "tensor")),
            P(("batch", "tensor")),
            P(("batch", "tensor")),
            P("batch", "tensor"),
            P("batch", "tensor"),
            P("tensor", "batch"),
            P(("batch", "tensor")),
        ),
        check_vma=False,
    )
```

time: 2520 us -> 1300 us (0.52)
  matrix products: 989 us -> 244 us
  blocking collectives: 420 us -> 42.4 us
  waiting for transfers between devices: 402 us -> 705 us
  local copies, waits for them, and re-layouts: 332 us -> 80.8 us
  other arithmetic: 297 us -> 53.8 us
  Pallas kernels: 0 us -> 124 us
  loops' own time: 28 us -> 0 us
    dot_general x24 -> x0, matrix products: 756 us -> none  [the longest x2 88.8 us: forward_transform(): first_re = jnp.einsum('ka,msab->mskb', cos_a, signal, precision=HIGH)]
    unnamed x2 -> x0, blocking collectives: 189 us -> none
    all_gather x2 -> x0, blocking collectives: 158 us -> none  [the longest x1 93.3 us: on_device(): lax.all_gather(short_kernel, ('batch', 'tensor'), axis=1, tiled=True)]
    another operation x40 -> x0, local copies, waits for them, and re-layouts: 142 us -> none
    unnamed x17, waiting for transfers between devices: 3.87 us -> 145 us
    all_to_all x5, waiting for transfers between devices: 77.3 us -> 207 us  [the longest x1 68.3 us: on_device(): lax.all_to_all(mixed_chan[:, :channels], 'tensor', split_axis=0, concat_a...]
    pallas_call x0 -> x2, Pallas kernels: none -> 124 us  [the longest x1 63.6 us: conv_backward(): pl.pallas_call(conv_backward_kernel, grid=(channels // LANES,), in_specs=...]
    all_gather x1, waiting for transfers between devices: 130 us -> 17 us  [on_device(): lax.all_gather(shards[2], 'tensor', axis=0, tiled=True)]
  transfers between devices with their start and end apart: 21 -> 20, of which waited for: 9 -> 13; matrix products, arithmetic and copies ran while one was open for 62% -> 24% of each run, Pallas kernels for 0% -> 10%
where the time goes in v1:
time: 1300 us
  waiting for transfers between devices  705 us (54%)
  matrix products  244 us (19%)
  Pallas kernels  124 us (10%)
  local copies, waits for them, and re-layouts  80.8 us (6%)
  other arithmetic  53.8 us (4%)
  blocking collectives  42.4 us (3%)
  starting transfers between devices  26.9 us (2%)
  between operations  18.8 us (1%)
    unnamed x17, waiting for transfers between devices  145 us
    reduce_scatter x2, waiting for transfers between devices, on_device(): lax.psum_scatter(lax.psum_scatter(grad.astype(bf16), 'tensor', scatter_di...  128 us
    reduce_scatter x1, waiting for transfers between devices, on_device(): lax.psum_scatter(jnp.concatenate([grad_in_full.astype(bf16), grad_out_ful...  108 us
    all_to_all x1, waiting for transfers between devices, on_device(): lax.all_to_all(mixed_chan[:, :channels], 'tensor', split_axis=0, concat_a...  68.3 us
    all_gather x1, waiting for transfers between devices, on_device(): lax.all_gather(jnp.concatenate([in_weight, out_weight, pad_lanes(small)],...  66.7 us
    pallas_call x1, Pallas kernels, conv_backward(): pl.pallas_call(conv_backward_kernel, grid=(channels // LANES,), in_specs=...  63.6 us
    all_to_all x2, waiting for transfers between devices, on_device(): lax.all_to_all(projected[:, n * width:(n + 1) * width].astype(bf16), 'ten...  61.3 us
    pallas_call x1, Pallas kernels, conv_forward(): pl.pallas_call(conv_forward_kernel, grid=(channels // LANES,), in_specs=[...  59.9 us
  transfers between devices with their start and end apart: 20, of which 13 were waited for; matrix products, arithmetic and copies ran while one was open for 24% of the time, Pallas kernels for 10%

profile of v1, /device:TPU:0, one launch (start us, length us, event | category | flops | bytes accessed | tf_op | source)
XLA Modules:
  0.0 1295.4 jit_solution(2518944637639678462)
XLA Ops:
  21.7 33.6 %all-gather.10.cloned.1.call-done = bf16[768,1536]{1,0:T(8,128)(2,1)} async-done(((bf16[48,1536]{1,0:T(8,128)(2,1)}), bf16[768,1536]{1,0:T(8,128)(2,1)}) %all-gather.10.cloned.1.call-update) | async-done | bytes 2359312 | tf_op jit(solution)/shard_map/all_gather | solution.py:430
  55.3 66.7 %all-gather.8.cloned.1.call-done = bf16[768,3200]{1,0:T(8,128)(2,1)} async-done(((bf16[24,3200]{1,0:T(8,128)(2,1)}), bf16[768,3200]{1,0:T(8,128)(2,1)}) %all-gather.8.cloned.1.call-update) | async-done | bytes 4915216 | tf_op jit(solution)/shard_map/all_gather | solution.py:419
  126.0 13.8 %fusion.36 = (bf16[2048,2304]{1,0:T(8,128)(2,1)S(1)}, f32[2048,2304]{1,0:T(8,128)}) fusion(f32[2304]{0:T(1024)} %add.132, bf16[768,3200]{1,0:T(8,128)(2,1)} %all-gather.8.cloned.1.call-done, bf16[2048,768]{0,1:T(8,128)(2,1)S(1)} %copy.116, f32[768]{0:T(1024)} %get-tuple-element.106, f32[768]{0:T(1024)} %get-tuple-element.107, ...), kind=kOutput, calls=%fused_computation.117 | convolution fusion | flops 7266631680 | bytes 35033088 | tf_op jit(solution)/shard_map/dot_general | solution.py:437
  160.8 25.1 %all-to-all-done = bf16[2048,2,384]{2,0,1:T(8,128)(2,1)} async-done(((bf16[2048,2,384]{2,0,1:T(8,128)(2,1)}), bf16[2048,2,384]{2,0,1:T(8,128)(2,1)}, u32[]{:S(2)}, u32[]{:S(2)}) %all-to-all-start) | async-done | bytes 3145760 | tf_op jit(solution)/shard_map/all_to_all | solution.py:440
  198.9 36.2 %all-to-all-done.1 = bf16[2048,2,384]{2,0,1:T(8,128)(2,1)} async-done(((bf16[2048,2,384]{2,0,1:T(8,128)(2,1)}), bf16[2048,2,384]{2,0,1:T(8,128)(2,1)}, u32[]{:S(2)}, u32[]{:S(2)}) %all-to-all-start.1) | async-done | bytes 3145760 | tf_op jit(solution)/shard_map/all_to_all | solution.py:440
  236.5 59.9 %conv_forward.1 = (bf16[32,128,384]{2,1,0:T(8,128)(2,1)}, bf16[64,128,384]{2,1,0:T(8,128)(2,1)}, bf16[64,128,384]{2,1,0:T(8,128)(2,1)}, f32[32,384]{1,0:T(8,128)}) custom-call(bf16[4096,384]{1,0:T(8,128)(2,1)} %bitcast.10.kern_ref, bf16[4096,384]{1,0:T(8,128)(2,1)} %bitcast.12.val_ref, f32[3,384]{1,0:T(4,128)} %get-tuple-element.145.taps_k, ...), custom_call_target="tpu_custom_call" | custom-call | flops 20937965568 | bytes 47185920 | tf_op jit(solution)/shard_map/conv_forward/pallas_call | solution.py:295
  302.7 68.3 %all-to-all-done.2 = bf16[2,2048,384]{2,1,0:T(8,128)(2,1)} async-done(((bf16[2,2048,384]{2,1,0:T(8,128)(2,1)}), bf16[2,2048,384]{2,1,0:T(8,128)(2,1)}, u32[]{:S(2)}, u32[]{:S(2)}) %all-to-all-start.2) | async-done | bytes 3145760 | tf_op jit(solution)/shard_map/all_to_all | solution.py:463
  389.2 16.8 %fusion.39 = f32[2048,3072]{1,0:T(8,128)} fusion(bf16[2048,768]{0,1:T(8,128)(2,1)S(1)} %add_convert_fusion, bf16[768,3072]{1,0:T(8,128)(2,1)} %all-gather.12.cloned.1.call-done), kind=kOutput, calls=%fused_computation.120 | convolution fusion | flops 9663676416 | bytes 33030144 | tf_op jit(solution)/shard_map/dot_general | solution.py:475
  406.0 15.7 %fusion.40 = f32[2048,3072]{1,0:T(8,128)} fusion(bf16[2048,768]{0,1:T(8,128)(2,1)S(1)} %add_convert_fusion, bf16[768,3072]{1,0:T(8,128)(2,1)} %all-gather.16.cloned.1.call-done), kind=kOutput, calls=%fused_computation.121 | convolution fusion | flops 9663676416 | bytes 33030144 | tf_op jit(solution)/shard_map/dot_general | solution.py:476
  421.7 17.0 %all-gather.20.cloned.1.call-done = bf16[3072,768]{0,1:T(8,128)(2,1)} async-done(((bf16[1536,768]{0,1:T(8,128)(2,1)}), bf16[3072,768]{0,1:T(8,128)(2,1)}) %all-gather.20.cloned.1.call-update) | async-done | bytes 4718608 | tf_op jit(solution)/shard_map/all_gather | solution.py:473
  438.7 38.9 %multiply_convert_fusion = (bf16[2048,3072]{1,0:T(8,128)(2,1)}, bf16[2048,3072]{1,0:T(8,128)(2,1)}, bf16[2048,3072]{1,0:T(8,128)(2,1)}) fusion(f32[2048,3072]{1,0:T(8,128)} %fusion.39, f32[2048,3072]{1,0:T(8,128)} %fusion.40, bf16[3072,768]{0,1:T(8,128)(2,1)} %all-gather.20.cloned.1.call-done, f32[2048,768]{1,0:T(8,128)} %param.23), kind=kOutput, calls=%fused_computation | convolution fusion | flops 9759621120 | bytes 99090432 | tf_op jit(solution)/shard_map/rd,fd->rf/dot_general | solution.py:482
  477.6 28.0 %convolution_convert_fusion = bf16[3072,768]{1,0:T(8,128)(2,1)} fusion(bf16[2048,3072]{1,0:T(8,128)(2,1)} %get-tuple-element.112, f32[2048,768]{1,0:T(8,128)} %param.23), kind=kOutput, calls=%fused_computation.39 | convolution fusion | flops 9667608576 | bytes 23592960 | tf_op jit(solution)/shard_map/rf,rd->fd/dot_general | solution.py:483
  512.4 14.4 %convolution_convert_fusion.1 = bf16[768,3072]{1,0:T(8,128)(2,1)} fusion(bf16[2048,768]{0,1:T(8,128)(2,1)S(1)} %add_convert_fusion, bf16[2048,3072]{1,0:T(8,128)(2,1)} %get-tuple-element.110), kind=kOutput, calls=%fused_computation.40 | convolution fusion | flops 9666035712 | bytes 20447232 | tf_op jit(solution)/shard_map/rd,rf->df/dot_general | solution.py:489
  526.9 16.5 %fusion.41 = f32[2048,768]{0,1:T(8,128)} fusion(bf16[2048,3072]{1,0:T(8,128)(2,1)} %get-tuple-element.111, bf16[768,3072]{1,0:T(8,128)(2,1)} %all-gather.12.cloned.1.call-done), kind=kOutput, calls=%fused_computation.122 | convolution fusion | flops 9663676416 | bytes 23592960 | tf_op jit(solution)/shard_map/rf,df->rd/dot_general | solution.py:490
  543.4 20.2 %multiply_reduce_fusion = (f32[768]{0:T(1024)S(1)}, f32[2048]{0:T(1024)S(1)}, f32[2048]{0:T(1024)S(1)}, f32[768]{0:T(1024)S(1)}, f32[2048,768]{0,1:T(8,128)}) fusion(f32[2048,768]{0,1:T(8,128)} %copy-done.2, f32[2048]{0:T(1024)S(1)} %copy-done.17, f32[2048]{0:T(1024)S(1)} %copy-done.13, f32[768]{0:T(1024)S(1)} %copy-done.23, f32[2048,768]{0,1:T(8,128)} %fusion.41, ...), kind=kOutput, calls=%fused_computation.27 | convolution fusion | flops 9679398912 | bytes 36217856 | tf_op jit(solution)/shard_map/rf,df->rd/dot_general | solution.py:492
  563.6 8.1 convert_reduce_fusion.2
  571.7 8.7 multiply_convert_fusion.4
  587.9 15.6 %convolution_convert_fusion.2 = bf16[768,3072]{1,0:T(8,128)(2,1)} fusion(bf16[2048,768]{0,1:T(8,128)(2,1)} %copy-done.8, bf16[2048,3072]{1,0:T(8,128)(2,1)} %get-tuple-element.111), kind=kOutput, calls=%fused_computation.41 | convolution fusion | flops 9666035712 | bytes 20447232 | tf_op jit(solution)/shard_map/rd,rf->df/dot_general | solution.py:488
  603.5 55.2 %all-to-all-done.3 = bf16[2048,2,384]{2,0,1:T(8,128)(2,1)} async-done(((bf16[2048,2,384]{2,0,1:T(8,128)(2,1)}), bf16[2048,2,384]{2,0,1:T(8,128)(2,1)}, u32[]{:S(2)}, u32[]{:S(2)}) %all-to-all-start.3) | async-done | bytes 3145760 | tf_op jit(solution)/shard_map/all_to_all | solution.py:513
  658.7 63.6 %conv_backward.1 = (bf16[4096,384]{1,0:T(8,128)(2,1)}, bf16[4096,384]{1,0:T(8,128)(2,1)}, f32[3,384]{1,0:T(4,128)}, f32[3,384]{1,0:T(4,128)}) custom-call(bf16[32,128,384]{2,1,0:T(8,128)(2,1)} %bitcast.22.grad_ref, bf16[4096,384]{1,0:T(8,128)(2,1)} %bitcast.10.kern_ref, bf16[4096,384]{1,0:T(8,128)(2,1)} %bitcast.12.val_ref, ...), custom_call_target="tpu_custom_call" | custom-call | flops 24159191040 | bytes 62914560 | tf_op jit(solution)/shard_map/conv_backward/pallas_call | solution.py:330
  722.4 42.4 %all_to_all.105 = bf16[2,2048,384]{2,1,0:T(8,128)(2,1)} all-to-all(bf16[2,2048,384]{2,1,0:T(8,128)(2,1)} %bitcast.117), channel_id=1, replica_groups=mesh['batch'=16,'tensor'=2] {'tensor'}, dimensions={0} | all-to-all | bytes 6291456 | tf_op jit(solution)/shard_map/all_to_all | solution.py:519
  771.9 7.6 convolution_convert_fusion.4
  782.7 22.0 %all-to-all-done.5 = bf16[2,2048,384]{2,1,0:T(8,128)(2,1)} async-done(((bf16[2,2048,384]{2,1,0:T(8,128)(2,1)}), bf16[2,2048,384]{2,1,0:T(8,128)(2,1)}, u32[]{:S(2)}, u32[]{:S(2)}) %all-to-all-start.5) | async-done | bytes 3145760 | tf_op jit(solution)/shard_map/all_to_all | solution.py:519
  811.1 12.4 fusion.38
  836.6 13.4 %convolution_convert_fusion.3 = bf16[768,2304]{1,0:T(8,128)(2,1)} fusion(bf16[2048,768]{0,1:T(8,128)(2,1)S(1)} %copy-done.1, f32[768]{0:T(1024)S(1)} %copy-done.31, f32[768]{0:T(1024)S(1)} %copy-done.21, f32[2048]{0:T(1024)S(1)} %copy-done.15, f32[2048]{0:T(1024)S(1)} %copy-done.11, bf16[2048,768]{1,0:T(8,128)(2,1)} %bitcast.106, ...), kind=kOutput, calls=%fused_computation.42 | convolution fusion | flops 7287275520 | bytes 16144384 | tf_op jit(solution)/shard_map/rd,rk->dk/dot_general | solution.py:523
  861.5 17.1 %convolution_add_fusion.2 = f32[2048,768]{0,1:T(8,128)} fusion(f32[2048,768]{0,1:T(8,128)} %copy-done.2, bf16[2048,3072]{1,0:T(8,128)(2,1)} %get-tuple-element.112, bf16[3072,768]{0,1:T(8,128)(2,1)} %all-gather.20.cloned.1.call-done), kind=kOutput, calls=%fused_computation.47 | convolution fusion | flops 9665249280 | bytes 29884416 | tf_op jit(solution)/shard_map/dot_general | solution.py:480
  885.2 7.7 fusion.12
  899.4 78.2 %all-reduce.6.cloned.1.call-done = f32[768,128]{0,1:T(8,128)} async-done(((f32[768,128]{0,1:T(8,128)}), f32[768,128]{0,1:T(8,128)}) %all-reduce.6.cloned.1.call-update) | async-done | bytes 393232
  981.3 107.7 %reduce-scatter.11.cloned.1.call-done = bf16[24,3072]{1,0:T(8,128)(2,1)} async-done(((bf16[768,3072]{1,0:T(8,128)(2,1)}), bf16[24,3072]{1,0:T(8,128)(2,1)}) %reduce-scatter.11.cloned.1.call-update) | async-done | bytes 147472 | tf_op jit(solution)/shard_map/reduce_scatter | solution.py:550
  1092.0 63.3 %reduce-scatter.23.cloned.1.call-done = bf16[48,1536]{1,0:T(8,128)(2,1)} async-done(((bf16[768,1536]{1,0:T(8,128)(2,1)}), bf16[48,1536]{1,0:T(8,128)(2,1)}) %reduce-scatter.23.cloned.1.call-update) | async-done | bytes 147472
  1157.3 63.6 %reduce-scatter.19.cloned.1.call-done = bf16[48,1536]{1,0:T(8,128)(2,1)} async-done(((bf16[768,1536]{1,0:T(8,128)(2,1)}), bf16[48,1536]{1,0:T(8,128)(2,1)}) %reduce-scatter.19.cloned.1.call-update) | async-done | bytes 147472 | tf_op jit(solution)/shard_map/reduce_scatter | solution.py:494
  1222.6 64.4 %reduce-scatter.15.cloned.1.call-done = bf16[48,1536]{1,0:T(8,128)(2,1)} async-done(((bf16[768,1536]{1,0:T(8,128)(2,1)}), bf16[48,1536]{1,0:T(8,128)(2,1)}) %reduce-scatter.15.cloned.1.call-update) | async-done | bytes 147472 | tf_op jit(solution)/shard_map/reduce_scatter | solution.py:494
  (212 shorter events, 154.6 us)
Async XLA Ops:
  7.2 48.1 %all-gather.10.cloned.1.call-start = ((), (), s32[]{:S(2)}) async-start(), calls=%async_computation.14 | async-start | bytes 2506752 | tf_op jit(solution)/shard_map/all_gather | solution.py:430
  7.9 114.0 %all-gather.8.cloned.1.call-start = ((), (), s32[]{:S(2)}) async-start(), calls=%async_computation.13 | async-start | bytes 5068800 | tf_op jit(solution)/shard_map/all_gather | solution.py:419
  15.7 176.1 %all-gather.14.cloned.1.call-start = ((), (), s32[]{:S(2)}) async-start(), calls=%async_computation.16 | async-start | bytes 2506752 | tf_op jit(solution)/shard_map/all_gather | solution.py:431
  16.5 285.2 %all-gather.18.cloned.1.call-start = ((), (), s32[]{:S(2)}) async-start(), calls=%async_computation.18 | async-start | bytes 2506752 | tf_op jit(solution)/shard_map/all_gather | solution.py:432
  17.0 372.1 %all-gather.12.cloned.1.call-start = ((), (), s32[]{:S(2)}) async-start(), calls=%async_computation.15 | async-start | bytes 7077888 | tf_op jit(solution)/shard_map/all_gather | solution.py:471
  20.3 359.6 %copy-start = (bf16[2048,768]{0,1:T(8,128)(2,1)}, bf16[2048,768]{0,1:T(8,128)(2,1)S(1)}, u32[]{:S(2)}) copy-start(bf16[2048,768]{0,1:T(8,128)(2,1)S(1)} %copy.116) | copy-start | bytes 9437188
  20.8 119.0 %copy-start.10 = (f32[2048]{0:T(1024)}, f32[2048]{0:T(1024)S(1)}, u32[]{:S(2)}) copy-start(f32[2048]{0:T(1024)S(1)} %broadcast_multiply_fusion.5) | copy-start | bytes 24580
  21.7 118.1 %copy-start.14 = (f32[2048]{0:T(1024)}, f32[2048]{0:T(1024)S(1)}, u32[]{:S(2)}) copy-start(f32[2048]{0:T(1024)S(1)} %add_rsqrt_fusion.1) | copy-start | bytes 24580
  143.9 42.0 %all-to-all-start = ((bf16[2048,2,384]{2,0,1:T(8,128)(2,1)}), bf16[2048,2,384]{2,0,1:T(8,128)(2,1)}, u32[]{:S(2)}, u32[]{:S(2)}) async-start(bf16[2048,2,384]{2,0,1:T(8,128)(2,1)} %bitcast.108), calls=%async_computation | async-start | bytes 6291456 | tf_op jit(solution)/shard_map/all_to_all | solution.py:440
  156.8 35.1 %copy-start.18 = (f32[128,128]{1,0:T(8,128)S(1)}, f32[128,128]{1,0:T(8,128)}, u32[]{:S(2)}) copy-start(f32[128,128]{1,0:T(8,128)} %constant.71.clone) | copy-start | bytes 196612
  156.8 35.1 %copy-start.19 = (f32[128,128]{1,0:T(8,128)S(1)}, f32[128,128]{1,0:T(8,128)}, u32[]{:S(2)}) copy-start(f32[128,128]{1,0:T(8,128)} %constant.72.clone) | copy-start | bytes 196612
  185.9 49.2 %all-to-all-start.1 = ((bf16[2048,2,384]{2,0,1:T(8,128)(2,1)}), bf16[2048,2,384]{2,0,1:T(8,128)(2,1)}, u32[]{:S(2)}, u32[]{:S(2)}) async-start(bf16[2048,2,384]{2,0,1:T(8,128)(2,1)} %bitcast.109), calls=%async_computation.1 | async-start | bytes 6291456 | tf_op jit(solution)/shard_map/all_to_all | solution.py:440
  191.1 214.9 %all-gather.16.cloned.1.call-start = ((), (), s32[]{:S(2)}) async-start(), calls=%async_computation.17 | async-start | bytes 7077888 | tf_op jit(solution)/shard_map/all_gather | solution.py:472
  296.4 74.6 %all-to-all-start.2 = ((bf16[2,2048,384]{2,1,0:T(8,128)(2,1)}), bf16[2,2048,384]{2,1,0:T(8,128)(2,1)}, u32[]{:S(2)}, u32[]{:S(2)}) async-start(bf16[2,2048,384]{2,1,0:T(8,128)(2,1)} %bitcast.116), calls=%async_computation.2 | async-start | bytes 6291456 | tf_op jit(solution)/shard_map/all_to_all | solution.py:463
  301.6 137.1 %all-gather.20.cloned.1.call-start = ((), (), s32[]{:S(2)}) async-start(), calls=%async_computation.19 | async-start | bytes 7077888 | tf_op jit(solution)/shard_map/all_gather | solution.py:473
  302.4 552.8 %reduce-scatter.21.cloned.1.call-start = ((), (), s32[]{:S(2)}) async-start(), calls=%async_computation.25 | async-start | bytes 7077888 | tf_op jit(solution)/shard_map/reduce_scatter | solution.py:495
  389.1 123.3 %copy-start.8 = (bf16[2048,768]{0,1:T(8,128)(2,1)}, bf16[2048,768]{0,1:T(8,128)(2,1)S(1)}, u32[]{:S(2)}) copy-start(bf16[2048,768]{0,1:T(8,128)(2,1)S(1)} %add_convert_fusion) | copy-start | bytes 9437188
  505.7 353.9 %reduce-scatter.17.cloned.1.call-start = ((), (), s32[]{:S(2)}) async-start(), calls=%async_computation.23 | async-start | bytes 7077888 | tf_op jit(solution)/shard_map/reduce_scatter | solution.py:495
  526.8 36.8 %slice-start = ((s8[6291456]{0:T(1024)(128)(4,1)}), s8[4194304]{0:T(1024)(128)(4,1)S(1)}, s32[]{:S(2)}) async-start(s8[6291456]{0:T(1024)(128)(4,1)} %bitcast.95), calls=%async_computation.28 | async-start | bytes 8388608
  526.9 44.8 %slice-start.2 = ((s8[6291456]{0:T(1024)(128)(4,1)}), s8[4194304]{0:T(1024)(128)(4,1)S(1)}, s32[]{:S(2)}) async-start(s8[6291456]{0:T(1024)(128)(4,1)} %bitcast.98), calls=%async_computation.30 | async-start | bytes 8388608
  543.4 20.2 %slice-start.1 = ((s8[6291456]{0:T(1024)(128)(4,1)}), s8[2097152]{0:T(1024)(128)(4,1)S(1)}, s32[]{:S(2)}) async-start(s8[6291456]{0:T(1024)(128)(4,1)} %bitcast.95), calls=%async_computation.29 | async-start | bytes 4194304
  543.4 28.3 %slice-start.3 = ((s8[6291456]{0:T(1024)(128)(4,1)}), s8[2097152]{0:T(1024)(128)(4,1)S(1)}, s32[]{:S(2)}) async-start(s8[6291456]{0:T(1024)(128)(4,1)} %bitcast.98), calls=%async_computation.31 | async-start | bytes 4194304
  580.4 230.7 %copy-start.4 = (bf16[2048,768]{1,0:T(8,128)(2,1)}, bf16[2048,768]{1,0:T(8,128)(2,1)S(1)}, u32[]{:S(2)}) copy-start(bf16[2048,768]{1,0:T(8,128)(2,1)S(1)} %get-tuple-element.115) | copy-start | bytes 9437188
  582.6 76.1 %all-to-all-start.3 = ((bf16[2048,2,384]{2,0,1:T(8,128)(2,1)}), bf16[2048,2,384]{2,0,1:T(8,128)(2,1)}, u32[]{:S(2)}, u32[]{:S(2)}) async-start(bf16[2048,2,384]{2,0,1:T(8,128)(2,1)} %bitcast.111), calls=%async_computation.3 | async-start | bytes 6291456 | tf_op jit(solution)/shard_map/all_to_all | solution.py:513
  587.9 273.6 %reduce-scatter.13.cloned.1.call-start = ((), (), s32[]{:S(2)}) async-start(), calls=%async_computation.21 | async-start | bytes 7077888 | tf_op jit(solution)/shard_map/reduce_scatter | solution.py:495
  722.3 48.3 %copy-start.20 = (f32[32,384]{1,0:T(8,128)S(1)}, f32[32,384]{1,0:T(8,128)}, u32[]{:S(2)}) copy-start(f32[32,384]{1,0:T(8,128)} %get-tuple-element.27.norm_ref) | copy-start | bytes 147460
  764.8 39.9 %all-to-all-start.5 = ((bf16[2,2048,384]{2,1,0:T(8,128)(2,1)}), bf16[2,2048,384]{2,1,0:T(8,128)(2,1)}, u32[]{:S(2)}, u32[]{:S(2)}) async-start(bf16[2,2048,384]{2,1,0:T(8,128)(2,1)} %bitcast.115), calls=%async_computation.5 | async-start | bytes 6291456 | tf_op jit(solution)/shard_map/all_to_all | solution.py:519
  770.0 207.6 %all-reduce.6.cloned.1.call-start = ((), (), s32[]{:S(2)}) async-start(), calls=%async_computation.27 | async-start | bytes 786432
  850.0 239.0 %reduce-scatter.11.cloned.1.call-start = ((), (), s32[]{:S(2)}) async-start(), calls=%async_computation.20 | async-start | bytes 4866048 | tf_op jit(solution)/shard_map/reduce_scatter | solution.py:550
  855.1 300.2 %reduce-scatter.23.cloned.1.call-start = ((), (), s32[]{:S(2)}) async-start(), calls=%async_computation.26 | async-start | bytes 2506752
  859.5 361.4 %reduce-scatter.19.cloned.1.call-start = ((), (), s32[]{:S(2)}) async-start(), calls=%async_computation.24 | async-start | bytes 2506752 | tf_op jit(solution)/shard_map/reduce_scatter | solution.py:494
  860.1 426.9 %reduce-scatter.15.cloned.1.call-start = ((), (), s32[]{:S(2)}) async-start(), calls=%async_computation.22 | async-start | bytes 2506752 | tf_op jit(solution)/shard_map/reduce_scatter | solution.py:494
  (28 other events, 185.6 us)
Sparse Core Ops, SparseCore 0:
  10.3 44.9 all-gather.9
  58.8 63.1 all-gather.7
  124.2 41.0 all-gather.13
  167.4 41.0 all-gather.17
  209.9 67.9 all-gather.11
  279.3 95.1 all-gather.15
  376.0 62.6 all-gather.19
  505.8 59.9 reduce-scatter.20
  568.2 93.7 reduce-scatter.16
  664.1 59.9 reduce-scatter.12
  850.1 127.4 all-reduce.5
  982.9 105.9 reduce-scatter.10
  1093.2 62.0 reduce-scatter.22
  1158.9 61.9 reduce-scatter.18
  1225.0 61.9 reduce-scatter.14

commit v2 on v1

v2 whole, which is shorter than its diff:
```python
import functools
import math

import jax
import jax.numpy as jnp
import numpy as np
from jax import lax
from jax.experimental import pallas as pl
from jax.experimental.pallas import tpu as pltpu
from jax.sharding import PartitionSpec as P

EPS = 1e-05
TINY = 1e-06
LANES = 128
INNER = 128
OCTET = 8
f32 = jnp.float32
bf16 = jnp.bfloat16


def first_stage(outer, level):
    part = outer >> level
    index = np.arange(part)
    angle = (index[:, None] + 0.5) * index[None, :] * (math.pi / part)
    block = np.stack([np.cos(angle), -np.sin(angle)], 1).reshape(2 * part, part)
    return np.kron(np.eye(1 << level), block)


def turn_angles(outer, level):
    part = outer >> level
    index = np.arange(outer) % part
    return (index[:, None] + 0.5) * np.arange(INNER)[None, :] * (math.pi / (part * INNER))


def conv_tables(bin_rows):
    outer = bin_rows // INNER
    eye = np.eye(OCTET)
    base = np.arange(INNER)[:, None] * np.arange(INNER)[None, :] % INNER * (2.0 * math.pi / INNER)
    ones, backs, twos, flips = ([], [], [], [])
    for level in range(3):
        first = first_stage(outer, level)
        ones.append(np.kron(first, eye))
        backs.append(np.kron(first.T / (bin_rows >> level), eye))
        angle = base[None] + turn_angles(outer, level)[:, None, :]
        upper = np.concatenate([np.cos(angle), np.sin(angle)], 2)
        lower = np.concatenate([-np.sin(angle), np.cos(angle)], 2)
        both = np.concatenate([upper, lower], 1)
        twos.append(both)
        flips.append(both.transpose(0, 2, 1))
    return tuple(
        jnp.asarray(np.stack(item).astype(np.float32).astype(bf16))
        for item in (ones, twos, flips, backs)
    )


def lay_out(meta, room_ref, joined_ref, count):
    outer = room_ref.shape[0]
    shift = int(math.log2(outer)) - meta[0]

    def row(chunk, carry):
        slot = lax.shift_right_logical(chunk, shift)
        within = chunk - lax.shift_left(slot, shift)
        room = meta[1 + count + slot] - within * INNER
        room_ref[pl.ds(chunk, 1), :] = jnp.full((1, LANES), room, jnp.int32)
        joined_ref[pl.ds(chunk, 1), :] = jnp.full((1, LANES), jnp.minimum(within, 1)).astype(f32)
        return carry

    lax.fori_loop(0, outer, row, 0)
    joined_ref[outer:, :] = jnp.zeros((OCTET, LANES), f32)
    left = lax.broadcasted_iota(jnp.int32, (outer, outer), 0)
    right = lax.broadcasted_iota(jnp.int32, (outer, outer), 1)
    same = lax.shift_right_logical(left, shift) == lax.shift_right_logical(right, shift)
    return same.astype(f32)


def shifted_back(now, before, iota):
    one = jnp.where(iota == 0, before[15:16], pltpu.roll(now, 1, 0))
    two = jnp.where(
        iota == 0, before[14:15], jnp.where(iota == 1, before[15:16], pltpu.roll(now, 2, 0))
    )
    return (one, two)


def load_chunk(ref, chunk, joined_row):
    now = ref[pl.ds(pl.multiple_of(chunk * INNER, INNER), INNER), :].astype(f32)
    at = pl.multiple_of(jnp.maximum(chunk * INNER - 16, 0), 16)
    before = ref[pl.ds(at, 16), :].astype(f32) * joined_row
    return (now, before)


def fill_rows(meta, pieces, target):
    rows = pieces[0].shape[0]
    for index, piece in enumerate(pieces):
        at = pl.multiple_of(meta[1 + index] * rows, rows)
        target[pl.ds(at, rows), :] = piece[...]


def conv_forward_kernel(
    count, meta, *refs
):
    kern_pieces, val_pieces, refs = (refs[:count], refs[count : 2 * count], refs[2 * count :])
    conv_forward_body(meta, kern_pieces, val_pieces, refs[6 : 6 + count], *refs[:6], *refs[6 + count :])


def conv_forward_body(
    meta, kern_pieces, val_pieces, outs, taps_k, taps_v, one_ref, two_ref, back_two_ref,
    back_one_ref,
    unit_ref, vspec_ref, norm_ref,
    kern_ref, val_ref, time_buf, mid_buf, low_buf, square_buf, room_ref, joined_ref,
):
    outer = kern_ref.shape[0] // INNER
    count = len(kern_pieces)
    same = lay_out(meta, room_ref, joined_ref, count)
    fill_rows(meta, kern_pieces, kern_ref)
    fill_rows(meta, val_pieces, val_ref)
    iota = lax.broadcasted_iota(jnp.int32, (INNER, LANES), 0)

    def prepare(chunk, carry):
        joined = joined_ref[pl.ds(chunk, 1), :]
        valid = iota < room_ref[pl.ds(chunk, 1), :]
        now, before = load_chunk(kern_ref, chunk, joined)
        one, two = shifted_back(now, before, iota)
        kern = jnp.where(valid, taps_k[0:1] * now + taps_k[1:2] * one + taps_k[2:3] * two, 0.0)
        time_buf[chunk, :, 0:LANES] = kern
        square_buf[pl.ds(chunk, 1), :] = jnp.sum(kern * kern, 0, keepdims=True)
        now, before = load_chunk(val_ref, chunk, joined)
        one, two = shifted_back(now, before, iota)
        val = jnp.where(valid, taps_v[0:1] * now + taps_v[1:2] * one + taps_v[2:3] * two, 0.0)
        time_buf[chunk, :, LANES:] = val
        return carry

    lax.fori_loop(0, outer, prepare, 0, unroll=4)
    total = jnp.dot(same, square_buf[...], precision=lax.Precision.HIGHEST)
    norm = jnp.sqrt(total + TINY)
    norm_ref[...] = norm
    square_buf[...] = 1.0 / norm

    def stage_one(pair, carry):
        at = pl.multiple_of(pair * 16, 16)
        halves = []
        for half in range(2):
            part = time_buf[:, pl.ds(at + half * OCTET, OCTET), :]
            part = part.reshape(outer * OCTET, 2 * LANES).astype(bf16)
            done = jnp.dot(one_ref[0], part, preferred_element_type=f32)
            halves.append(done.reshape(2 * outer, OCTET, 2 * LANES))
        mid_buf[:, pl.ds(at, 16), :] = jnp.concatenate(halves, 1).astype(bf16)
        return carry

    lax.fori_loop(0, INNER // 16, stage_one, 0, unroll=8)

    def stage_two(kk, carry):
        row = pl.multiple_of(kk * 2, 2)
        part = mid_buf[pl.ds(row, 2)].reshape(2 * INNER, 2 * LANES)
        spec = jnp.dot(two_ref[0, kk], part, preferred_element_type=f32)
        inverse = square_buf[pl.ds(kk, 1), :]
        unit_re = spec[:INNER, :LANES] * inverse
        unit_im = spec[INNER:, :LANES] * inverse
        val_re = spec[:INNER, LANES:]
        val_im = spec[INNER:, LANES:]
        unit_ref[row] = unit_re.astype(bf16)
        unit_ref[row + 1] = unit_im.astype(bf16)
        vspec_ref[row] = val_re.astype(bf16)
        vspec_ref[row + 1] = val_im.astype(bf16)
        power = unit_re * unit_re + unit_im * unit_im
        made = jnp.concatenate([power * val_re, power * val_im], 0).astype(bf16)
        back = jnp.dot(back_two_ref[0, kk], made, preferred_element_type=f32)
        low_buf[row] = back[:INNER]
        low_buf[row + 1] = back[INNER:]
        return carry

    lax.fori_loop(0, outer, stage_two, 0, unroll=16)
    spot = lax.broadcasted_iota(jnp.int32, (outer, 16, LANES), 1)

    def back_one(pair, carry):
        at = pl.multiple_of(pair * 16, 16)
        halves = []
        for half in range(2):
            part = low_buf[:, pl.ds(at + half * OCTET, OCTET), :]
            part = part.reshape(2 * outer * OCTET, LANES).astype(bf16)
            done = jnp.dot(back_one_ref[0], part, preferred_element_type=f32)
            halves.append(done.reshape(outer, OCTET, LANES))
        whole = jnp.concatenate(halves, 1)
        valid = spot + at < room_ref[...][:, None, :]
        whole = jnp.where(valid, whole, 0.0).astype(bf16)
        part = outer // count
        for index in range(count):
            for role in range(count):

                @pl.when(meta[1 + index] == role)
                def _(index=index, role=role):
                    outs[role][:, pl.ds(at, 16), :] = whole[index * part : (index + 1) * part]

        return carry

    lax.fori_loop(0, INNER // 16, back_one, 0, unroll=8)


def conv_backward_kernel(count, meta, *refs):
    groups = [refs[n * count : (n + 1) * count] for n in range(3)]
    refs = refs[3 * count :]
    conv_backward_body(meta, *groups, refs[9 : 9 + count], *refs[:9], *refs[9 + count :])


def conv_backward_body(
    meta, grad_pieces, kern_pieces, val_pieces, outs, unit_ref, vspec_ref, norm_ref, taps_k, taps_v,
    one_ref, two_ref, back_two_ref, back_one_ref,
    dtaps_k, dtaps_v,
    kern_ref, val_ref, grad_buf, time_buf, mid_buf, low_buf, dots_buf, inv_buf,
    room_ref, joined_ref,
):
    outer = kern_ref.shape[0] // INNER
    count = len(kern_pieces)
    same = lay_out(meta, room_ref, joined_ref, count)
    part = outer // count
    fill_rows(meta, kern_pieces, kern_ref)
    fill_rows(meta, val_pieces, val_ref)
    for index, piece in enumerate(grad_pieces):
        grad_buf[pl.ds(meta[1 + index] * part, part)] = piece[...]
    iota = lax.broadcasted_iota(jnp.int32, (INNER, LANES), 0)
    spot = lax.broadcasted_iota(jnp.int32, (outer, 16, LANES), 1)

    def stage_one(pair, carry):
        at = pl.multiple_of(pair * 16, 16)
        whole = grad_buf[:, pl.ds(at, 16), :].astype(f32)
        whole = jnp.where(spot + at < room_ref[...][:, None, :], whole, 0.0)
        halves = []
        for half in range(2):
            part = whole[:, half * OCTET : (half + 1) * OCTET]
            part = part.reshape(outer * OCTET, LANES).astype(bf16)
            done = jnp.dot(one_ref[0], part, preferred_element_type=f32)
            halves.append(done.reshape(2 * outer, OCTET, LANES))
        mid_buf[:, pl.ds(at, 16), :] = jnp.concatenate(halves, 1).astype(bf16)
        return carry

    lax.fori_loop(0, INNER // 16, stage_one, 0, unroll=8)

    def stage_two(kk, carry):
        row = pl.multiple_of(kk * 2, 2)
        part = mid_buf[pl.ds(row, 2)].reshape(2 * INNER, LANES)
        spec = jnp.dot(two_ref[0, kk], part, preferred_element_type=f32)
        grad_re = spec[:INNER]
        grad_im = spec[INNER:]
        unit_re = unit_ref[row].astype(f32)
        unit_im = unit_ref[row + 1].astype(f32)
        val_re = vspec_ref[row].astype(f32)
        val_im = vspec_ref[row + 1].astype(f32)
        power = unit_re * unit_re + unit_im * unit_im
        slope = 2.0 * (grad_re * val_re + grad_im * val_im)
        dots_buf[pl.ds(kk, 1), :] = jnp.sum(power * slope, 0, keepdims=True)
        upper = jnp.concatenate([power * grad_re, slope * unit_re], 1)
        lower = jnp.concatenate([power * grad_im, slope * unit_im], 1)
        made = jnp.concatenate([upper, lower], 0).astype(bf16)
        back = jnp.dot(back_two_ref[0, kk], made, preferred_element_type=f32)
        low_buf[row] = back[:INNER]
        low_buf[row + 1] = back[INNER:]
        return carry

    lax.fori_loop(0, outer, stage_two, 0, unroll=16)

    def back_one(octet, carry):
        at = pl.multiple_of(octet * OCTET, OCTET)
        part = low_buf[:, pl.ds(at, OCTET), :]
        part = part.reshape(2 * outer * OCTET, 2 * LANES).astype(bf16)
        done = jnp.dot(back_one_ref[0], part, preferred_element_type=f32)
        time_buf[:, pl.ds(at, OCTET), :] = done.reshape(outer, OCTET, 2 * LANES)
        return carry

    lax.fori_loop(0, INNER // OCTET, back_one, 0, unroll=16)
    inv_buf[...] = 1.0 / norm_ref[...]
    share = same / (jnp.sum(same, 1, keepdims=True) * INNER)
    dots_buf[...] = jnp.dot(share, dots_buf[...], precision=lax.Precision.HIGHEST)

    def shifted_ahead(now, after):
        one = jnp.where(iota == INNER - 1, after[0:1], pltpu.roll(now, INNER - 1, 0))
        two = jnp.where(
            iota == INNER - 1,
            after[1:2],
            jnp.where(iota == INNER - 2, after[0:1], pltpu.roll(now, INNER - 2, 0)),
        )
        return (one, two)

    def finish(step, carry):
        after_k, after_v, sums = carry
        chunk = outer - 1 - step
        joined = joined_ref[pl.ds(chunk, 1), :]
        ahead = joined_ref[pl.ds(chunk + 1, 1), :]
        valid = iota < room_ref[pl.ds(chunk, 1), :]
        inverse = inv_buf[pl.ds(chunk, 1), :]
        along = dots_buf[pl.ds(chunk, 1), :]
        slot = meta[1 + chunk // part]
        rows = pl.ds(pl.multiple_of(lax.rem(chunk, part) * INNER, INNER), INNER)
        now, before = load_chunk(kern_ref, chunk, joined)
        one, two = shifted_back(now, before, iota)
        unit = (taps_k[0:1] * now + taps_k[1:2] * one + taps_k[2:3] * two) * inverse
        grad = jnp.where(valid, (time_buf[chunk, :, LANES:] - unit * along) * inverse, 0.0)
        ahead_one, ahead_two = shifted_ahead(grad, after_k * ahead)
        d_kern = (
            taps_k[0:1] * grad + taps_k[1:2] * ahead_one + taps_k[2:3] * ahead_two
        ).astype(bf16)
        made = [jnp.sum(grad * item, 0, keepdims=True) for item in (now, one, two)]
        after_k = grad[:OCTET]
        now, before = load_chunk(val_ref, chunk, joined)
        one, two = shifted_back(now, before, iota)
        grad = jnp.where(valid, time_buf[chunk, :, :LANES], 0.0)
        ahead_one, ahead_two = shifted_ahead(grad, after_v * ahead)
        d_val = (
            taps_v[0:1] * grad + taps_v[1:2] * ahead_one + taps_v[2:3] * ahead_two
        ).astype(bf16)
        for role in range(count):

            @pl.when(slot == role)
            def _(role=role):
                outs[role][0, rows, :] = d_kern
                outs[role][1, rows, :] = d_val

        made += [jnp.sum(grad * item, 0, keepdims=True) for item in (now, one, two)]
        after_v = grad[:OCTET]
        return (after_k, after_v, tuple(a + b for a, b in zip(sums, made)))

    zero = jnp.zeros((OCTET, LANES), f32)
    start = (zero, zero, tuple(jnp.zeros((1, LANES), f32) for _ in range(6)))
    _, _, sums = lax.fori_loop(0, outer, finish, start, unroll=4)
    for index in range(3):
        dtaps_k[index : index + 1, :] = sums[index]
        dtaps_v[index : index + 1, :] = sums[3 + index]


def level_spec(shape):
    zeros = (0,) * (len(shape) - 1)
    return pl.BlockSpec(
        (1,) + shape[1:], lambda c, meta: (meta[0],) + zeros, pipeline_mode=pl.Buffered(1)
    )


def lane_spec(rows, start=0):
    return pl.BlockSpec((rows, LANES), lambda c, meta: (0, c + start))


def cube_spec(depth, rows):
    return pl.BlockSpec((depth, rows, LANES), lambda c, meta: (0, 0, c))


def conv_forward(pieces, meta, taps_k, taps_v, tables):
    count = len(pieces)
    rows, channels = pieces[0].shape[0], pieces[0].shape[1] // 2
    bin_rows = rows * count
    outer = bin_rows // INNER
    blocks = channels // LANES
    return pl.pallas_call(
        functools.partial(conv_forward_kernel, count),
        grid_spec=pltpu.PrefetchScalarGridSpec(
            num_scalar_prefetch=1,
            grid=(blocks,),
            in_specs=[lane_spec(rows)] * count
            + [lane_spec(rows, blocks)] * count
            + [lane_spec(3), lane_spec(3)]
            + [level_spec(item.shape) for item in tables],
            out_specs=[cube_spec(outer // count, INNER)] * count
            + [
                cube_spec(2 * outer, INNER),
                cube_spec(2 * outer, INNER),
                lane_spec(outer),
            ],
            scratch_shapes=[
                pltpu.VMEM((bin_rows, LANES), bf16),
                pltpu.VMEM((bin_rows, LANES), bf16),
                pltpu.VMEM((outer, INNER, 2 * LANES), f32),
                pltpu.VMEM((2 * outer, INNER, 2 * LANES), bf16),
                pltpu.VMEM((2 * outer, INNER, LANES), f32),
                pltpu.VMEM((outer, LANES), f32),
                pltpu.VMEM((outer, LANES), jnp.int32),
                pltpu.VMEM((outer + OCTET, LANES), f32),
            ],
        ),
        out_shape=[jax.ShapeDtypeStruct((outer // count, INNER, channels), bf16)] * count
        + [
            jax.ShapeDtypeStruct((2 * outer, INNER, channels), bf16),
            jax.ShapeDtypeStruct((2 * outer, INNER, channels), bf16),
            jax.ShapeDtypeStruct((outer, channels), f32),
        ],
        compiler_params=pltpu.CompilerParams(vmem_limit_bytes=56 << 20),
        cost_estimate=pl.CostEstimate(
            flops=26 * channels * bin_rows * 512,
            bytes_accessed=30 * bin_rows * channels,
            transcendentals=0,
        ),
        name="conv_forward",
    )(meta, *pieces, *pieces, taps_k, taps_v, *tables)


def conv_backward(grads, pieces, meta, unit, vspec, norm, taps_k, taps_v, tables):
    count = len(pieces)
    rows, channels = pieces[0].shape[0], pieces[0].shape[1] // 2
    bin_rows = rows * count
    outer = bin_rows // INNER
    blocks = channels // LANES
    part = outer // count
    rows_out = pl.BlockSpec((2, rows, LANES), lambda c, meta: (0, 0, c))
    return pl.pallas_call(
        functools.partial(conv_backward_kernel, count),
        grid_spec=pltpu.PrefetchScalarGridSpec(
            num_scalar_prefetch=1,
            grid=(blocks,),
            in_specs=[cube_spec(part, INNER)] * count
            + [lane_spec(rows)] * count
            + [lane_spec(rows, blocks)] * count
            + [cube_spec(2 * outer, INNER), cube_spec(2 * outer, INNER), lane_spec(outer)]
            + [lane_spec(3), lane_spec(3)]
            + [level_spec(item.shape) for item in tables],
            out_specs=[rows_out] * count + [lane_spec(3), lane_spec(3)],
            scratch_shapes=[
                pltpu.VMEM((bin_rows, LANES), bf16),
                pltpu.VMEM((bin_rows, LANES), bf16),
                pltpu.VMEM((outer, INNER, LANES), bf16),
                pltpu.VMEM((outer, INNER, 2 * LANES), f32),
                pltpu.VMEM((2 * outer, INNER, LANES), bf16),
                pltpu.VMEM((2 * outer, INNER, 2 * LANES), f32),
                pltpu.VMEM((outer, LANES), f32),
                pltpu.VMEM((outer, LANES), f32),
                pltpu.VMEM((outer, LANES), jnp.int32),
                pltpu.VMEM((outer + OCTET, LANES), f32),
            ],
        ),
        out_shape=[jax.ShapeDtypeStruct((2, rows, channels), bf16)] * count
        + [
            jax.ShapeDtypeStruct((3, channels), f32),
            jax.ShapeDtypeStruct((3, channels), f32),
        ],
        compiler_params=pltpu.CompilerParams(vmem_limit_bytes=56 << 20),
        cost_estimate=pl.CostEstimate(
            flops=channels * bin_rows,
            bytes_accessed=bin_rows * channels,
            transcendentals=0,
        ),
        name="conv_backward",
    )(
        meta,
        *(item.reshape(part, INNER, channels) for item in grads),
        *pieces,
        *pieces,
        unit,
        vspec,
        norm,
        taps_k,
        taps_v,
        *tables,
    )


def norm_parts(values, gain, bias):
    row_mean = jnp.mean(values, -1, keepdims=True)
    centred = values - row_mean
    row_var = jnp.mean(centred * centred, -1, keepdims=True)
    inverse = lax.rsqrt(row_var + EPS)
    normed = centred * inverse
    return (normed * gain + bias, normed, inverse)


def norm_back(grad_out, normed, inverse, gain):
    scaled = grad_out * gain
    centre_term = jnp.mean(scaled, -1, keepdims=True)
    slope_term = jnp.mean(scaled * normed, -1, keepdims=True)
    return inverse * (scaled - centre_term - normed * slope_term)


ROW_TILE = 1024
TURN = 256


def dot_nt(left, right):
    return lax.dot_general(left, right, (((1,), (1,)), ((), ())), preferred_element_type=f32)


def feed_kernel(
    normed_ref, cot_ref, gate_ref, up_ref, down_ref,
    out_ref, second_ref, packed_ref,
    normed_t, cot_t, sums,
):
    step = pl.program_id(0)
    rows = normed_ref.shape[0]
    tile = packed_ref.shape[-1]
    chunk = min(ROW_TILE, rows)

    @pl.when(step == 0)
    def _():
        out_ref[...] = jnp.zeros_like(out_ref)
        second_ref[...] = jnp.zeros_like(second_ref)

        def turn(index, carry):
            at = pl.multiple_of(index * TURN, TURN)
            normed_t[:, pl.ds(at, TURN)] = normed_ref[pl.ds(at, TURN), :].T
            cot_t[:, pl.ds(at, TURN)] = cot_ref[pl.ds(at, TURN), :].T
            return carry

        lax.fori_loop(0, rows // TURN, turn, 0)

    sums[...] = jnp.zeros_like(sums)

    def work(index, carry):
        at = pl.multiple_of(index * chunk, chunk)
        here = pl.ds(at, chunk)
        normed = normed_ref[here, :]
        cot = cot_ref[here, :]
        gate = jnp.dot(normed, gate_ref[0], preferred_element_type=f32)
        up = jnp.dot(normed, up_ref[0], preferred_element_type=f32)
        d_hidden = jnp.dot(cot, down_ref[0], preferred_element_type=f32)
        sigmoid = 1.0 / (1.0 + jnp.exp(-gate))
        silu = gate * sigmoid
        hidden = (silu * up).astype(bf16)
        d_up = (d_hidden * silu).astype(bf16)
        d_gate = (d_hidden * up * sigmoid * (1.0 + gate * (1.0 - sigmoid))).astype(bf16)
        out_ref[here, :] += dot_nt(hidden, down_ref[0])
        second_ref[here, :] += dot_nt(d_gate, gate_ref[0]) + dot_nt(d_up, up_ref[0])
        sums[0] += jnp.dot(normed_t[:, here], d_gate, preferred_element_type=f32)
        sums[1] += jnp.dot(normed_t[:, here], d_up, preferred_element_type=f32)
        sums[2] += jnp.dot(cot_t[:, here], hidden, preferred_element_type=f32)
        return carry

    lax.fori_loop(0, rows // chunk, work, 0)
    for kind in range(3):
        packed_ref[0, :, kind] = sums[kind].reshape(-1, *packed_ref.shape[3:]).astype(bf16)

def feed_forward(normed, cot, weights, hidden_cols, batch):
    rows, width = normed.shape
    parts = weights.shape[0]
    tile = 512 if hidden_cols % 512 == 0 else hidden_cols
    tiles = hidden_cols // tile

    def block(kind):
        return pl.BlockSpec((1, width, tile), lambda n: (n // tiles, 0, kind * tiles + n % tiles))
    whole = pl.BlockSpec((rows, width), lambda n: (0, 0), pipeline_mode=pl.Buffered(1))
    return pl.pallas_call(
        feed_kernel,
        grid=(parts * tiles,),
        in_specs=[whole, whole, block(0), block(1), block(2)],
        out_specs=[whole, whole, pl.BlockSpec((1, batch, 3, width // batch, tile), lambda n: (n // tiles, 0, 0, 0, n % tiles))],
        out_shape=[
            jax.ShapeDtypeStruct((rows, width), f32),
            jax.ShapeDtypeStruct((rows, width), f32),
            jax.ShapeDtypeStruct((parts, batch, 3, width // batch, hidden_cols), bf16),
        ],
        scratch_shapes=[
            pltpu.VMEM((width, rows), bf16),
            pltpu.VMEM((width, rows), bf16),
            pltpu.VMEM((3, width, tile), f32),
        ],
        compiler_params=pltpu.CompilerParams(vmem_limit_bytes=60 << 20),
        cost_estimate=pl.CostEstimate(
            flops=18 * rows * width * hidden_cols * parts,
            bytes_accessed=18 * rows * width + 12 * parts * width * hidden_cols,
            transcendentals=0,
        ),
        name="feed_forward",
    )(normed, cot, weights, weights, weights)


BACK_TILE = 512


def norm_again(values):
    row_mean = jnp.mean(values, -1, keepdims=True)
    centred = values - row_mean
    inverse = lax.rsqrt(jnp.mean(centred * centred, -1, keepdims=True) + EPS)
    return (centred * inverse, inverse)


def row_sum(values):
    return jnp.sum(values, 0, keepdims=True)


def place_halves(core, write, own, other):
    for index in range(2):

        @pl.when(core == index)
        def _(index=index):
            write(index, own)
            write(1 - index, other)


def mixer_back_kernel(
    core_ref, second_ref, mlp_ref, middle_ref, cot_ref, gated_ref, queries_ref, own_ref, got_ref,
    normed_ref, out_weight_ref, gain_ref,
    out_ref, low_ref, grad_ref, d_q_ref, d_own_ref, d_send_ref, wide_ref, sums_ref,
    sum_q, sum_out,
):
    step = pl.program_id(0)
    half = own_ref.shape[1]
    width = 2 * half

    @pl.when(step == 0)
    def _():
        sum_q[...] = jnp.zeros_like(sum_q)
        sum_out[...] = jnp.zeros_like(sum_out)
        sums_ref[...] = jnp.zeros_like(sums_ref)

    middle = middle_ref[...]
    out = middle + mlp_ref[...]
    out_ref[...] = out
    low_ref[...] = out.astype(bf16)
    hat, inverse = norm_again(middle)
    d_second = second_ref[...]
    grad = cot_ref[...].astype(f32) + norm_back(d_second, hat, inverse, gain_ref[...])
    grad_ref[...] = grad
    d_mix = grad.astype(bf16)
    d_gated = dot_nt(d_mix, out_weight_ref[...])
    mixed = jnp.concatenate([own_ref[...], got_ref[...]], 1).astype(f32)
    d_q = (d_gated * mixed).astype(bf16)
    d_q_ref[...] = d_q
    d_mixed = (d_gated * queries_ref[...]).astype(bf16)
    d_own_ref[...] = d_mixed[:, :half]
    d_send_ref[...] = d_mixed[:, half:]
    sum_q[...] += jnp.dot(normed_ref[...].T, d_q, preferred_element_type=f32)
    sum_out[...] += jnp.dot(gated_ref[...].T, d_mix, preferred_element_type=f32)
    sums_ref[0:1] += row_sum(d_second * hat)
    sums_ref[1:2] += row_sum(d_second)
    sums_ref[2:3] += row_sum(d_mix.astype(f32))
    sums_ref[3:4] += row_sum(d_q.astype(f32))

    @pl.when(step == pl.num_programs(0) - 1)
    def _():
        core = core_ref[0]

        def write_q(index, value):
            wide_ref[:, index * half : (index + 1) * half] = value.astype(bf16)

        def write_out(index, value):
            wide_ref[index * half : (index + 1) * half, width:] = value.astype(bf16)

        place_halves(core, write_q, sum_q[:, :half], sum_q[:, half:])
        place_halves(core, write_out, sum_out[:half], sum_out[half:])


def mixer_back(
    core, second, mlp, middle, cot, gated, queries, own, got, normed, out_weight, gain
):
    rows, width = middle.shape
    half = width // 2
    tile = min(BACK_TILE, rows)

    def rows_of(columns):
        return pl.BlockSpec((tile, columns), lambda n, core: (n, 0))

    def whole(shape):
        return pl.BlockSpec(shape, lambda n, core: (0, 0))

    wide, narrow = (rows_of(width), rows_of(half))
    return pl.pallas_call(
        mixer_back_kernel,
        grid_spec=pltpu.PrefetchScalarGridSpec(
            num_scalar_prefetch=1,
            grid=(rows // tile,),
            in_specs=[wide] * 6 + [narrow, narrow, wide, whole((width, width)), whole((1, width))],
            out_specs=[wide] * 4 + [narrow, narrow, whole((width, 2 * width)), whole((8, width))],
            scratch_shapes=[
                pltpu.VMEM((width, width), f32),
                pltpu.VMEM((width, width), f32),
            ],
        ),
        out_shape=[
            jax.ShapeDtypeStruct((rows, width), f32),
            jax.ShapeDtypeStruct((rows, width), bf16),
            jax.ShapeDtypeStruct((rows, width), f32),
            jax.ShapeDtypeStruct((rows, width), bf16),
            jax.ShapeDtypeStruct((rows, half), bf16),
            jax.ShapeDtypeStruct((rows, half), bf16),
            jax.ShapeDtypeStruct((width, 2 * width), bf16),
            jax.ShapeDtypeStruct((8, width), f32),
        ],
        compiler_params=pltpu.CompilerParams(vmem_limit_bytes=56 << 20),
        cost_estimate=pl.CostEstimate(
            flops=6 * rows * width * width, bytes_accessed=40 * rows * width, transcendentals=0
        ),
        name="mixer_back",
    )(core, second, mlp, middle, cot, gated, queries, own, got, normed, out_weight, gain)


def entry_back_kernel(
    core_ref, d_q_ref, own_ref, got_ref, normed_ref, rows_ref, grad_ref,
    q_ref, k_ref, v_ref, gain_ref,
    out_ref, low_ref, pair_ref, sums_ref,
    total,
):
    step = pl.program_id(0)
    half = own_ref.shape[2]
    width = 2 * half

    @pl.when(step == 0)
    def _():
        total[...] = jnp.zeros_like(total)
        sums_ref[...] = jnp.zeros_like(sums_ref)

    kern = jnp.concatenate([own_ref[0], got_ref[0]], 1)
    val = jnp.concatenate([own_ref[1], got_ref[1]], 1)
    d_first = (
        dot_nt(d_q_ref[...], q_ref[...]) + dot_nt(kern, k_ref[...]) + dot_nt(val, v_ref[...])
    )
    hat, inverse = norm_again(rows_ref[...].astype(f32))
    grad = grad_ref[...] + norm_back(d_first, hat, inverse, gain_ref[...])
    out_ref[...] = grad
    low_ref[...] = grad.astype(bf16)
    turned = normed_ref[...].T
    total[:, :width] += jnp.dot(turned, kern, preferred_element_type=f32)
    total[:, width:] += jnp.dot(turned, val, preferred_element_type=f32)
    sums_ref[0:1] += row_sum(d_first * hat)
    sums_ref[1:2] += row_sum(d_first)
    sums_ref[2:3] += row_sum(kern.astype(f32))
    sums_ref[3:4] += row_sum(val.astype(f32))

    @pl.when(step == pl.num_programs(0) - 1)
    def _():
        for base in (0, width):

            def write(index, value, base=base):
                pair_ref[:, base + index * half : base + (index + 1) * half] = value.astype(bf16)

            place_halves(
                core_ref[0],
                write,
                total[:, base : base + half],
                total[:, base + half : base + width],
            )


def entry_back(core, d_q, own, got, normed, rows_in, grad, q_weight, k_weight, v_weight, gain):
    rows, width = grad.shape
    half = width // 2
    tile = min(BACK_TILE, rows)
    wide = pl.BlockSpec((tile, width), lambda n, core: (n, 0))
    pairs = pl.BlockSpec((2, tile, half), lambda n, core: (0, n, 0))

    def whole(shape):
        return pl.BlockSpec(shape, lambda n, core: (0, 0))

    return pl.pallas_call(
        entry_back_kernel,
        grid_spec=pltpu.PrefetchScalarGridSpec(
            num_scalar_prefetch=1,
            grid=(rows // tile,),
            in_specs=[wide, pairs, pairs, wide, wide, wide]
            + [whole((width, width))] * 3
            + [whole((1, width))],
            out_specs=[wide, wide, whole((width, 2 * width)), whole((8, width))],
            scratch_shapes=[pltpu.VMEM((width, 2 * width), f32)],
        ),
        out_shape=[
            jax.ShapeDtypeStruct((rows, width), f32),
            jax.ShapeDtypeStruct((rows, width), bf16),
            jax.ShapeDtypeStruct((width, 2 * width), bf16),
            jax.ShapeDtypeStruct((8, width), f32),
        ],
        compiler_params=pltpu.CompilerParams(vmem_limit_bytes=56 << 20),
        cost_estimate=pl.CostEstimate(flops=0, bytes_accessed=rows * width, transcendentals=0),
        name="entry_back",
    )(core, d_q, own, got, normed, rows_in, grad, q_weight, k_weight, v_weight, gain)


MESH = pl.DeviceIdType.MESH


def opening_kernel(
    rows_ref, lengths_ref, kern_ref, val_ref,
    rows_out, lengths_out, kern_out, val_out,
    send_sem, recv_sem, local_sem,
):
    b = lax.axis_index("batch")
    x = lax.axis_index("tensor")
    z, y, c = (b // 4, lax.rem(b // 2, 2), lax.rem(b, 2))

    def device(z, y, c, x):
        return (z * 4 + y * 2 + c, x)

    far = [lax.rem(z + k, 4) for k in (1, 2, 3)]
    greeted = [device(z, y, c, 1 - x), device(z, 1 - y, c, x), device(z, y, 1 - c, x)]
    greeted += [device(z, y, 1 - c, 1 - x)] + [device(other, y, c, x) for other in far]
    barrier = pltpu.get_barrier_semaphore()
    for other in greeted:
        pl.semaphore_signal(barrier, inc=1, device_id=other, device_id_type=MESH)
    pl.semaphore_wait(barrier, len(greeted))

    def remote(source, target, slot, other):
        return pltpu.make_async_remote_copy(
            src_ref=source,
            dst_ref=target,
            send_sem=send_sem.at[slot],
            recv_sem=recv_sem.at[slot],
            device_id=other,
            device_id_type=MESH,
        )

    turned = c != x
    cross = device(z, y, 1 - c, 1 - x)
    swaps = [remote(rows_ref, rows_out, 0, cross), remote(lengths_ref, lengths_out, 1, cross)]
    def first_steps(source, target, slot, by_z):
        own = pltpu.make_async_copy(source, target.at[z, y, c, x], local_sem.at[slot - 2])
        own.start()
        base = 2 + (slot - 2) * 6
        if by_z:
            copies = [
                remote(source, target.at[z, y, c, x], base + n, device(far[n], y, c, x))
                for n in range(3)
            ]
        else:
            copies = [remote(source, target.at[z, y, c, x], base, device(z, y, c, 1 - x))]
        for item in copies:
            item.start()
        return [own] + copies

    kern_first = first_steps(kern_ref, kern_out, 2, False)
    val_first = first_steps(val_ref, val_out, 3, True)

    @pl.when(turned)
    def _():
        for item in swaps:
            item.start()

    def finish(copies):
        for item in copies:
            item.wait()

    finish(kern_first)
    kern_second = [remote(kern_out.at[z, y, c], kern_out.at[z, y, c], 3, device(z, 1 - y, c, x))]
    kern_second[0].start()
    finish(val_first)
    val_second = [
        remote(val_out.at[:, y, c, x], val_out.at[:, y, c, x], 11, device(z, 1 - y, c, x))
    ]
    val_second[0].start()
    finish(kern_second)
    kern_third = [
        remote(kern_out.at[z, :, c], kern_out.at[z, :, c], 4 + n, device(far[n], y, c, x))
        for n in range(3)
    ]
    for item in kern_third:
        item.start()
    finish(val_second)
    val_third = [
        remote(val_out.at[:, :, c, x], val_out.at[:, :, c, x], 12, device(z, y, c, 1 - x))
    ]
    val_third[0].start()
    finish(kern_third)
    kern_last = [remote(kern_out.at[:, :, c], kern_out.at[:, :, c], 7, device(z, y, 1 - c, x))]
    kern_last[0].start()
    finish(val_third)
    val_last = [remote(val_out.at[:, :, c], val_out.at[:, :, c], 13, device(z, y, 1 - c, x))]
    val_last[0].start()
    finish(kern_last)
    finish(val_last)

    @pl.when(turned)
    def _():
        finish(swaps)


def opening(rows, lengths, kern, val):
    anywhere = pl.BlockSpec(memory_space=pl.ANY)
    rows_out, lengths_out, kern_out, val_out = pl.pallas_call(
        opening_kernel,
        in_specs=[anywhere] * 4,
        out_specs=[anywhere] * 4,
        out_shape=[
            jax.ShapeDtypeStruct(rows.shape, rows.dtype),
            jax.ShapeDtypeStruct(lengths.shape, lengths.dtype),
            jax.ShapeDtypeStruct((4, 2, 2, 2) + kern.shape, bf16),
            jax.ShapeDtypeStruct((4, 2, 2, 2) + val.shape, bf16),
        ],
        scratch_shapes=[
            pltpu.SemaphoreType.DMA((14,)),
            pltpu.SemaphoreType.DMA((14,)),
            pltpu.SemaphoreType.DMA((2,)),
        ],
        compiler_params=pltpu.CompilerParams(collective_id=1, has_side_effects=True),
        name="opening",
    )(rows, lengths, kern, val)
    return (
        rows_out,
        lengths_out,
        kern_out.reshape(32 * kern.shape[0], kern.shape[1]),
        val_out.reshape(32 * val.shape[0], val.shape[1]),
    )


def closing_kernel(
    grad_ref, wide_ref, small_ref, pair_ref,
    grad_out, first_out, second_out,
    first_own, first_core, first_far, first_y, first_x, first_sum, first_half, first_one,
    second_own, second_core, second_y, second_far, second_x, second_sum, second_half, second_one,
    send_sem, recv_sem, local_sem,
):
    b = lax.axis_index("batch")
    x = lax.axis_index("tensor")
    z, y, c = (b // 4, lax.rem(b // 2, 2), lax.rem(b, 2))
    wide = wide_ref.shape[-1]

    def device(z, y, c, x):
        return (z * 4 + y * 2 + c, x)

    far = [lax.rem(z + k, 4) for k in (1, 2, 3)]
    greeted = [device(z, y, c, 1 - x), device(z, 1 - y, c, x), device(z, y, 1 - c, x)]
    greeted += [device(z, y, 1 - c, 1 - x)] + [device(other, y, c, x) for other in far]
    barrier = pltpu.get_barrier_semaphore()
    for other in greeted:
        pl.semaphore_signal(barrier, inc=1, device_id=other, device_id_type=MESH)
    pl.semaphore_wait(barrier, len(greeted))

    def remote(source, target, slot, other):
        return pltpu.make_async_remote_copy(
            src_ref=source,
            dst_ref=target,
            send_sem=send_sem.at[slot],
            recv_sem=recv_sem.at[slot],
            device_id=other,
            device_id_type=MESH,
        )

    def begin(copies):
        for item in copies:
            item.start()
        return copies

    def finish(copies):
        for item in copies:
            item.wait()

    turned = c != x
    swap = remote(grad_ref, grad_out, 0, device(z, y, 1 - c, 1 - x))
    mate = device(z, y, 1 - c, x)
    beside = device(z, 1 - y, c, x)
    across = device(z, y, c, 1 - x)
    left = pl.ds(0, wide)
    right = pl.ds(wide, small_ref.shape[-1])
    second_c = begin(
        [
            remote(pair_ref.at[:, :, 1 - c], second_core, 1, mate),
            pltpu.make_async_copy(pair_ref.at[:, :, c], second_own, local_sem.at[0]),
        ]
    )
    first_c = begin(
        [
            remote(wide_ref.at[:, :, 1 - c], first_core.at[:, :, :, :, left], 2, mate),
            remote(small_ref.at[:, :, 1 - c], first_core.at[:, :, :, :, right], 3, mate),
            pltpu.make_async_copy(
                wide_ref.at[:, :, c], first_own.at[:, :, :, :, left], local_sem.at[1]
            ),
            pltpu.make_async_copy(
                small_ref.at[:, :, c], first_own.at[:, :, :, :, right], local_sem.at[2]
            ),
        ]
    )

    @pl.when(turned)
    def _():
        swap.start()

    def join(target, own, got):
        def step(index, carry):
            target[index] = (own[index].astype(f32) + got[index].astype(f32)).astype(bf16)
            return carry

        lax.fori_loop(0, 4, step, 0)

    finish(second_c)
    join(second_sum, second_own, second_core)
    second_b = begin([remote(second_sum.at[:, 1 - y], second_y, 4, beside)])
    finish(first_c)
    join(first_sum, first_own, first_core)
    first_z = begin(
        [
            remote(first_sum.at[far[n]], first_far.at[n], 5 + n, device(far[n], y, c, x))
            for n in range(3)
        ]
    )
    finish(second_b)

    def join_y(index, carry):
        second_half[index] = (
            second_sum[index, y].astype(f32) + second_y[index].astype(f32)
        ).astype(bf16)
        return carry

    lax.fori_loop(0, 4, join_y, 0)
    second_z = begin(
        [
            remote(second_half.at[far[n]], second_far.at[n], 8 + n, device(far[n], y, c, x))
            for n in range(3)
        ]
    )
    finish(first_z)
    first_half[...] = (
        first_sum[z].astype(f32)
        + first_far[0].astype(f32)
        + first_far[1].astype(f32)
        + first_far[2].astype(f32)
    ).astype(bf16)
    first_b = begin([remote(first_half.at[1 - y], first_y, 11, beside)])
    finish(second_z)
    second_one[...] = (
        second_half[z].astype(f32)
        + second_far[0].astype(f32)
        + second_far[1].astype(f32)
        + second_far[2].astype(f32)
    ).astype(bf16)
    second_a = begin([remote(second_one.at[1 - x], second_x, 12, across)])
    finish(first_b)
    first_one[...] = (first_half[y].astype(f32) + first_y[...].astype(f32)).astype(bf16)
    first_a = begin([remote(first_one.at[1 - x], first_x, 13, across)])
    finish(second_a)
    second_out[...] = second_one[x].astype(f32) + second_x[...].astype(f32)
    finish(first_a)
    first_out[...] = first_one[x].astype(f32) + first_x[...].astype(f32)

    @pl.when(turned)
    def _():
        swap.wait()


def closing(grad, wide, small, pair):
    def cube(array):
        return array.astype(bf16).reshape(4, 2, 2, 2, array.shape[0] // 32, array.shape[1])

    rows = wide.shape[0] // 32
    first = wide.shape[1] + small.shape[1]
    second = pair.shape[1]
    anywhere = pl.BlockSpec(memory_space=pl.ANY)
    inside = pl.BlockSpec(memory_space=pltpu.VMEM)

    def room(*lead):
        return pltpu.VMEM(lead, bf16)

    return pl.pallas_call(
        closing_kernel,
        in_specs=[anywhere] * 4,
        out_specs=[anywhere, inside, inside],
        out_shape=[
            jax.ShapeDtypeStruct(grad.shape, bf16),
            jax.ShapeDtypeStruct((rows, first), f32),
            jax.ShapeDtypeStruct((rows, second), f32),
        ],
        scratch_shapes=[
            room(4, 2, 2, rows, first),
            room(4, 2, 2, rows, first),
            room(3, 2, 2, rows, first),
            room(2, rows, first),
            room(rows, first),
            room(4, 2, 2, rows, first),
            room(2, 2, rows, first),
            room(2, rows, first),
            room(4, 2, 2, rows, second),
            room(4, 2, 2, rows, second),
            room(4, 2, rows, second),
            room(3, 2, rows, second),
            room(rows, second),
            room(4, 2, 2, rows, second),
            room(4, 2, rows, second),
            room(2, rows, second),
            pltpu.SemaphoreType.DMA((14,)),
            pltpu.SemaphoreType.DMA((14,)),
            pltpu.SemaphoreType.DMA((3,)),
        ],
        compiler_params=pltpu.CompilerParams(
            collective_id=2, has_side_effects=True, vmem_limit_bytes=40 << 20
        ),
        cost_estimate=pl.CostEstimate(flops=0, bytes_accessed=0, transcendentals=0),
        name="closing",
    )(grad, cube(wide), cube(small), cube(pair))


def pad_lanes(array):
    extra = -array.shape[-1] % LANES
    if extra == 0:
        return array
    return jnp.pad(array, ((0, 0),) * (array.ndim - 1) + ((0, extra),))


BOTH = ("batch", "tensor")
SPLIT = ("tensor", "batch")


class Grid:
    def __init__(self, shape):
        self.batch = shape["batch"]
        self.tensor = shape["tensor"]
        self.paired = self.tensor == 2 and self.batch % 2 == 0
        self.cubed = self.tensor == 2 and self.batch == 16
        self.b = lax.axis_index("batch")
        self.t = lax.axis_index("tensor")
        self.core = lax.rem(self.b, 2)

    def send(self, array, move):
        count = self.batch * self.tensor
        pairs = []
        for source in range(count):
            b, t = move(source // self.tensor, source % self.tensor)
            if b * self.tensor + t != source:
                pairs.append((source, b * self.tensor + t))
        return lax.ppermute(array, BOTH, pairs)

    def to_bins(self, array):
        if not self.paired:
            return array
        got = self.send(array, lambda b, t: ((b & ~1) | t, b & 1))
        return jnp.where(self.core == self.t, array, got)

    def from_bins(self, array, low):
        if not self.paired:
            return array
        got = self.send(low, lambda b, t: ((b & ~1) | t, b & 1))
        return jnp.where(self.core == self.t, array, got.astype(f32))

    def other_core(self, array):
        return self.send(array, lambda b, t: (b ^ 1, t))


def on_device(
    shape,
    activations,
    cotangent,
    buckets,
    lengths,
    first_gain,
    first_bias,
    in_weight,
    in_bias,
    short_kernel,
    short_value,
    out_weight,
    out_bias,
    second_gain,
    second_bias,
    gate_weight,
    up_weight,
    down_weight,
):
    grid = Grid(shape)
    width = activations.shape[1]
    shard_rows = in_weight.shape[0]
    block_rows, hidden_cols = gate_weight.shape
    parts = 2 if grid.paired else grid.tensor
    channels = width // parts
    turned = grid.paired

    bin_index = ((grid.b // 2) * 2 + grid.t) if grid.paired else grid.b
    part_index = grid.core if grid.paired else grid.t
    bucket_here = buckets[bin_index]

    small = jnp.concatenate(
        [
            first_gain[:, None],
            first_bias[:, None],
            out_bias[:, None],
            second_gain[:, None],
            second_bias[:, None],
            short_kernel.T,
            short_value.T,
            in_bias.reshape(shard_rows, 3),
        ],
        1,
    )
    k_shard = jnp.concatenate([in_weight[:, width : 2 * width], pad_lanes(small)], 1)
    v_shard = in_weight[:, 2 * width :]
    if grid.cubed:
        rows_bf, seq_lengths, k_full, v_full = opening(activations, lengths, k_shard, v_shard)
        rows_bf = jnp.where(grid.core == grid.t, activations, rows_bf)
        seq_lengths = jnp.where(grid.core == grid.t, lengths, seq_lengths)
    else:
        rows_bf = grid.to_bins(activations)
        seq_lengths = grid.to_bins(lengths)
        k_full = lax.all_gather(k_shard, BOTH, axis=0, tiled=True)
        v_full = lax.all_gather(v_shard, BOTH, axis=0, tiled=True)
    seq_lengths = seq_lengths[0]
    late_rows = jnp.concatenate([in_weight[:, :width], out_weight], 0).reshape(block_rows, -1)
    late = lax.all_gather(
        jnp.concatenate([gate_weight, up_weight, down_weight.T, late_rows], 1),
        SPLIT,
        axis=0,
        tiled=True,
    ).reshape(grid.tensor, grid.batch * block_rows, -1)

    def own_first(array, axis):
        if not turned:
            return array
        return jnp.where(grid.core == 0, array, jnp.roll(array, width // 2, axis))

    def unpick(array):
        held = array.reshape(grid.tensor, grid.batch, 2, shard_rows, width)
        return [held[:, :, n].transpose(1, 0, 2, 3).reshape(width, width) for n in (0, 1)]

    rows_small = k_full[:, width : width + 14].astype(f32).T
    gain_one, bias_one, out_shift, gain_two, bias_two = (rows_small[n] for n in range(5))
    in_shift = rows_small[11:14].T.reshape(3, width)
    q_shift, k_shift, v_shift = (own_first(in_shift[n], 0) for n in range(3))
    tap_rows = own_first(rows_small[5:11], 1)
    chan_start = jnp.int32(0) if turned else grid.t * channels

    def part_of(array, axis):
        return lax.dynamic_slice_in_dim(array, chan_start, channels, axis)

    short_k = pad_lanes(part_of(tap_rows[0:3], 1))
    short_v = pad_lanes(part_of(tap_rows[3:6], 1))
    k_weight = own_first(k_full[:, :width], 1)
    v_weight = own_first(v_full, 1)

    rows_in = rows_bf.astype(f32)
    first_out, first_hat, first_inv = norm_parts(rows_in, gain_one, bias_one)
    normed_first = first_out.astype(bf16)
    rows_here = rows_in.shape[0]

    def project(weight, shift):
        return jnp.dot(normed_first, weight, preferred_element_type=f32) + shift

    if turned:
        send_weight = jnp.concatenate([k_weight[:, channels:], v_weight[:, channels:]], 1)
        send_shift = jnp.concatenate([k_shift[channels:], v_shift[channels:]])
        own_weight = jnp.concatenate([k_weight[:, :channels], v_weight[:, :channels]], 1)
        own_shift = jnp.concatenate([k_shift[:channels], v_shift[:channels]])
        kv_send = project(send_weight, send_shift).astype(bf16)
        kv_got = grid.other_core(kv_send)
        kv_own = project(own_weight, own_shift).astype(bf16)
        pieces = [kv_own, kv_got]
        place = [grid.core, 1 - grid.core]
    else:
        kv_weight = jnp.concatenate([k_weight, v_weight], 1)
        kv_shift = jnp.concatenate([k_shift, v_shift])
        kv = project(kv_weight, kv_shift).astype(bf16)
        halves = [
            pad_lanes(lax.all_to_all(item, "tensor", split_axis=1, concat_axis=0, tiled=True))
            for item in (kv[:, :width], kv[:, width:])
        ]
        pieces = [jnp.concatenate(halves, 1)]
        place = [jnp.int32(0)]
    bin_rows = pieces[0].shape[0] * len(pieces)
    tables = conv_tables(bin_rows)
    meta = jnp.concatenate([jnp.stack([bucket_here] + place), seq_lengths]).astype(jnp.int32)
    *mixed_chan, unit_spec, value_spec, norms = conv_forward(
        pieces, meta, short_k, short_v, tables
    )
    norm_part = jnp.sum(norms[:, :channels], 0) / (bin_rows // INNER) * jnp.left_shift(
        jnp.int32(1), bucket_here
    ).astype(f32)
    if turned:
        mixed_own = mixed_chan[0].reshape(rows_here, channels)
        mixed_got = grid.other_core(mixed_chan[1]).reshape(rows_here, channels)
        mixed = jnp.concatenate([mixed_own, mixed_got], 1).astype(f32)
    else:
        mixed = lax.all_to_all(
            mixed_chan[0].reshape(bin_rows, -1)[:, :channels],
            "tensor",
            split_axis=0,
            concat_axis=1,
            tiled=True,
        ).astype(f32)

    q_weight, out_full = unpick(late[:, :, 3 * hidden_cols :])
    q_weight = own_first(q_weight, 1)
    out_full = own_first(out_full, 0)
    queries = project(q_weight, q_shift)
    gated = (queries * mixed).astype(bf16)
    middle = rows_in + jnp.dot(gated, out_full, preferred_element_type=f32) + out_shift
    second_out, second_hat, second_inv = norm_parts(middle, gain_two, bias_two)
    normed_second = second_out.astype(bf16)
    cot_low = grid.to_bins(cotangent.astype(bf16))
    mlp_out, d_second, packed = feed_forward(
        normed_second, cot_low, late, hidden_cols, grid.batch
    )
    mlp_sum = lax.psum_scatter(
        packed.reshape(-1, hidden_cols), SPLIT, scatter_dimension=0, tiled=True
    ).astype(f32)

    def natural(array, axis):
        return own_first(array, axis)

    if turned:
        core = grid.core.astype(jnp.int32)[None]
        out_here, out_low, grad_middle, d_queries, d_own, d_send, wide_grad, sums = mixer_back(
            core,
            d_second,
            mlp_out,
            middle,
            cot_low,
            gated,
            queries,
            mixed_own,
            mixed_got,
            normed_first,
            out_full,
            gain_two[None],
        )
        grad_gain_two, grad_bias_two, grad_out_shift, grad_q_shift = (sums[n] for n in range(4))
        d_mixed_pieces = [d_own, grid.other_core(d_send)]
    else:
        out_here = middle + mlp_out
        second_hat, second_inv = norm_parts(middle, gain_two, bias_two)[1:]
        grad_middle = cot_low.astype(f32) + norm_back(d_second, second_hat, second_inv, gain_two)
        grad_gain_two = jnp.sum(d_second * second_hat, 0)
        grad_bias_two = jnp.sum(d_second, 0)
        d_mix = grad_middle.astype(bf16)
        d_gated = jnp.einsum("re,de->rd", d_mix, out_full, preferred_element_type=f32)
        d_mixed = (d_gated * queries).astype(bf16)
        d_mixed_pieces = [
            pad_lanes(lax.all_to_all(d_mixed, "tensor", split_axis=1, concat_axis=0, tiled=True))
        ]
        d_queries = (d_gated * mixed).astype(bf16)
        grad_out_full = jnp.einsum("rd,re->de", gated, d_mix, preferred_element_type=f32)
        grad_out_shift = jnp.sum(d_mix.astype(f32), 0)
        grad_q = jnp.einsum("rd,rk->dk", normed_first, d_queries, preferred_element_type=f32)
        grad_q_shift = jnp.sum(d_queries.astype(f32), 0)
        wide_grad = jnp.concatenate([grad_q, grad_out_full], 1)
    *d_pieces, d_taps_k, d_taps_v = conv_backward(
        d_mixed_pieces, pieces, meta, unit_spec, value_spec, norms, short_k, short_v, tables
    )
    if turned:
        grad_here, grad_low, pair_grad, sums = entry_back(
            core,
            d_queries,
            d_pieces[0],
            grid.other_core(d_pieces[1]),
            normed_first,
            rows_bf,
            grad_middle,
            q_weight,
            k_weight,
            v_weight,
            gain_one[None],
        )
        grad_gain_one, grad_bias_one, grad_k_shift, grad_v_shift = (sums[n] for n in range(4))
    else:
        d_kv = jnp.concatenate(
            [
                lax.all_to_all(
                    d_pieces[0][n][:, :channels], "tensor", split_axis=0, concat_axis=1, tiled=True
                )
                for n in (0, 1)
            ],
            1,
        )
        kv_weight = jnp.concatenate([k_weight, v_weight], 1)
        d_first = jnp.einsum(
            "rk,dk->rd", d_queries, q_weight, preferred_element_type=f32
        ) + jnp.einsum("rk,dk->rd", d_kv, kv_weight, preferred_element_type=f32)
        grad_here = grad_middle + norm_back(d_first, first_hat, first_inv, gain_one)
        grad_low = grad_here.astype(bf16)
        grad_gain_one = jnp.sum(d_first * first_hat, 0)
        grad_bias_one = jnp.sum(d_first, 0)
        pair_grad = jnp.einsum("rd,rk->dk", normed_first, d_kv, preferred_element_type=f32)
        grad_k_shift = jnp.sum(d_kv[:, :width].astype(f32), 0)
        grad_v_shift = jnp.sum(d_kv[:, width:].astype(f32), 0)
    chan_rows = jnp.concatenate(
        [d_taps_k[:, :channels], d_taps_v[:, :channels], norm_part[None]], 0
    )
    chan_full = lax.dynamic_update_slice(
        jnp.zeros((7, width), f32), chan_rows, (jnp.int32(0), chan_start)
    )
    turned_rows = jnp.concatenate(
        [chan_full, grad_q_shift[None], grad_k_shift[None], grad_v_shift[None]], 0
    )
    turned_rows = natural(turned_rows, 1)
    small_rows = jnp.concatenate(
        [
            grad_gain_one[None],
            grad_bias_one[None],
            grad_out_shift[None],
            grad_gain_two[None],
            grad_bias_two[None],
            turned_rows[:7],
            turned_rows[7:].reshape(width, 3).T,
        ],
        0,
    )
    small_grad = pad_lanes(small_rows.T)
    if turned:
        out_rows = grid.from_bins(out_here, out_low)
    else:
        out_rows = out_here
    if grid.cubed:
        swapped, first_sum, pair_sum = closing(grad_low, wide_grad, small_grad, pair_grad)
        grad_activations = jnp.where(grid.core == grid.t, grad_here, swapped.astype(f32))
        wide_sum = first_sum[:, : 2 * width]
        small_sum = first_sum[:, 2 * width :]
    else:
        grad_activations = grid.from_bins(grad_here, grad_low)
        total = lax.psum_scatter(
            jnp.concatenate([item.astype(bf16) for item in (wide_grad, small_grad, pair_grad)], 1),
            BOTH,
            scatter_dimension=0,
            tiled=True,
        ).astype(f32)
        wide_sum = total[:, : 2 * width]
        small_sum = total[:, 2 * width : 2 * width + small_grad.shape[1]]
        pair_sum = total[:, 2 * width + small_grad.shape[1] :]
    seq_count = jnp.sum(jnp.left_shift(jnp.ones_like(buckets), buckets)).astype(f32)
    return (
        out_rows,
        grad_activations,
        small_sum[:, 0],
        small_sum[:, 1],
        jnp.concatenate([wide_sum[:, :width], pair_sum], 1),
        small_sum[:, 12:15].reshape(3 * shard_rows),
        small_sum[:, 5:8].T,
        small_sum[:, 8:11].T,
        wide_sum[:, width:],
        small_sum[:, 2],
        small_sum[:, 3],
        small_sum[:, 4],
        mlp_sum[:block_rows],
        mlp_sum[block_rows : 2 * block_rows],
        mlp_sum[2 * block_rows :].T,
        small_sum[:, 11] / seq_count,
    )


def solution(mesh):
    return jax.shard_map(
        functools.partial(on_device, dict(mesh.shape)),
        mesh=mesh,
        in_specs=(
            P(("batch", "tensor"), None),
            P(("batch", "tensor"), None),
            P(),
            P("batch", None),
            P(("batch", "tensor")),
            P(("batch", "tensor")),
            P(("batch", "tensor"), None),
            P(("batch", "tensor")),
            P(None, ("batch", "tensor")),
            P(None, ("batch", "tensor")),
            P(("batch", "tensor"), None),
            P(("batch", "tensor")),
            P(("batch", "tensor")),
            P(("batch", "tensor")),
            P("batch", "tensor"),
            P("batch", "tensor"),
            P("tensor", "batch"),
        ),
        out_specs=(
            P(("batch", "tensor"), None),
            P(("batch", "tensor"), None),
            P(("batch", "tensor")),
            P(("batch", "tensor")),
            P(("batch", "tensor"), None),
            P(("batch", "tensor")),
            P(None, ("batch", "tensor")),
            P(None, ("batch", "tensor")),
            P(("batch", "tensor"), None),
            P(("batch", "tensor")),
            P(("batch", "tensor")),
            P(("batch", "tensor")),
            P("batch", "tensor"),
            P("batch", "tensor"),
            P("tensor", "batch"),
            P(("batch", "tensor")),
        ),
        check_vma=False,
    )
```

time: 1300 us -> 506 us (0.39)
  waiting for transfers between devices: 705 us -> 0.98 us
  Pallas kernels: 124 us -> 372 us
  matrix products: 244 us -> 19.3 us
  blocking collectives: 42.4 us -> 0 us
  local copies, waits for them, and re-layouts: 80.8 us -> 38.6 us
  other arithmetic: 53.8 us -> 38.4 us
  starting transfers between devices: 26.9 us -> 11.5 us
    pallas_call x2 -> x7, Pallas kernels: 124 us -> 372 us  [the longest x1 106 us: feed_forward(): pl.pallas_call(feed_kernel, grid=(parts * tiles,), in_specs=[whole, whole...]
    reduce_scatter x6 -> x1, waiting for transfers between devices: 236 us -> 0.01 us  [on_device(): lax.psum_scatter(packed.reshape(-1, hidden_cols), SPLIT, scatter_dimensio...]
    dot_general x14 -> x3, matrix products: 239 us -> 16.2 us  [project(): return jnp.dot(normed_first, weight, preferred_element_type=f32) + shift]
    all_to_all x5 -> x0, waiting for transfers between devices: 207 us -> none  [the longest x1 68.3 us: on_device(): lax.all_to_all(mixed_chan[:, :channels], 'tensor', split_axis=0, concat_a...]
    unnamed x17 -> x2, waiting for transfers between devices: 145 us -> 0.03 us
    all_gather x7 -> x1, waiting for transfers between devices: 117 us -> 0.01 us  [on_device(): lax.all_gather(jnp.concatenate([gate_weight, up_weight, down_weight.T, la...]
    all_to_all x1 -> x0, blocking collectives: 42.4 us -> none  [on_device(): lax.all_to_all(item[:, :channels], 'tensor', split_axis=0, concat_axis=1,...]
    all_to_all x5 -> x0, starting transfers between devices: 26.1 us -> none  [the longest x2 10.4 us: on_device(): lax.all_to_all(projected[:, n * width:(n + 1) * width].astype(bf16), 'ten...]
  transfers between devices with their start and end apart: 20 -> 8, of which waited for: 13 -> 1; matrix products, arithmetic and copies ran while one was open for 24% -> 13% of each run, Pallas kernels for 10% -> 54%
where the time goes in v2:
time: 506 us; the launch traced here: 497 us
  Pallas kernels  372 us (74%)
  local copies, waits for them, and re-layouts  38.6 us (8%)
  other arithmetic  38.4 us (8%)
  matrix products  19.3 us (4%)
  between operations  16.2 us (3%)
  starting transfers between devices  11.5 us (2%)
    pallas_call x1, Pallas kernels, feed_forward(): pl.pallas_call(feed_kernel, grid=(parts * tiles,), in_specs=[whole, whole...  106 us
    pallas_call x1, Pallas kernels, opening(): pl.pallas_call(opening_kernel, in_specs=[anywhere] * 4, out_specs=[anywhe...  68.9 us
    pallas_call x1, Pallas kernels, closing(): pl.pallas_call(closing_kernel, in_specs=[anywhere] * 4, out_specs=[anywhe...  67.9 us
    pallas_call x1, Pallas kernels, conv_backward(): pl.pallas_call(functools.partial(conv_backward_kernel, count), grid_spec=...  44.9 us
    pallas_call x1, Pallas kernels, conv_forward(): pl.pallas_call(functools.partial(conv_forward_kernel, count), grid_spec=p...  36.3 us
    pallas_call x1, Pallas kernels, mixer_back(): pl.pallas_call(mixer_back_kernel, grid_spec=pltpu.PrefetchScalarGridSpec(...  26.8 us
    pallas_call x1, Pallas kernels, entry_back(): pl.pallas_call(entry_back_kernel, grid_spec=pltpu.PrefetchScalarGridSpec(...  21.5 us
    unnamed x60, local copies, waits for them, and re-layouts  17 us
  transfers between devices with their start and end apart: 8, of which 1 were waited for; matrix products, arithmetic and copies ran while one was open for 13% of the time, Pallas kernels for 54%

profile of v2, /device:TPU:0, one launch (start us, length us, event | category | flops | bytes accessed | tf_op | source)
XLA Modules:
  0.0 497.4 jit_solution(12035481551736909369)
XLA Ops:
  7.2 1.4 fusion.30
  8.7 1.9 maximum_maximum_fusion
  17.5 68.9 %opening.1 = (bf16[2048,768]{1,0:T(8,128)(2,1)}, s32[1,4]{1,0:T(1,128)}, bf16[4,2,2,2,24,896]{5,4,3,2,1,0:T(8,128)(2,1)}, bf16[4,2,2,2,24,768]{5,4,3,2,1,0:T(8,128)(2,1)}) custom-call(bf16[2048,768]{1,0:T(8,128)(2,1)} %rows_ref.1, s32[1,4]{1,0:T(1,128)} %lengths_ref.1, bf16[24,896]{1,0:T(8,128)(2,1)} %fusion.15.kern_ref, ...), custom_call_target="tpu_custom_call" | custom-call | tf_op jit(solution)/shard_map/opening/pallas_call | solution.py:856
  89.5 2.9 convert_reduce_fusion
  98.4 1.3 fusion.5.normed_ref
  99.7 4.0 add_convert_fusion.1
  104.1 2.0 convert_element_type.53
  106.1 2.3 collective-permute-start.2
  110.0 1.2 pad_add_fusion.meta
  111.9 6.7 %add_convert_fusion.2.refs_0_.refs_2_.refs_4_ = bf16[2048,768]{1,0:T(8,128)(2,1)} fusion(bf16[2048,768]{1,0:T(8,128)(2,1)} %copy-done.5, f32[768]{0:T(1024)S(1)} %pad_maximum_fusion.2, bf16[768,384]{1,0:T(8,128)(2,1)} %get-tuple-element.134, bf16[768,384]{1,0:T(8,128)(2,1)} %get-tuple-element.132), kind=kOutput, calls=%fused_computation.16 | convolution fusion | flops 2421424128 | bytes 7474176 | tf_op jit(solution)/shard_map/dot_general | solution.py:1208
  118.6 36.3 %conv_forward.1 = (bf16[16,128,384]{2,1,0:T(8,128)(2,1)}, bf16[16,128,384]{2,1,0:T(8,128)(2,1)}, bf16[64,128,384]{2,1,0:T(8,128)(2,1)}, bf16[64,128,384]{2,1,0:T(8,128)(2,1)}, f32[32,384]{1,0:T(8,128)}) custom-call(s32[7]{0:T(128)} %pad_add_fusion.meta, bf16[2048,768]{1,0:T(8,128)(2,1)} %add_convert_fusion.2.refs_0_.refs_2_.refs_4_, ...), custom_call_target="tpu_custom_call" | custom-call | flops 20937965568 | bytes 47185920 | tf_op jit(solution)/shard_map/conv_forward/pallas_call | solution.py:349
  155.0 4.9 broadcast_select_fusion.cot_ref
  159.8 1.8 slice.340
  163.0 1.9 copy-done.6
  165.4 5.6 %multiply_convert_fusion = (bf16[2048,768]{1,0:T(8,128)(2,1)S(1)}, f32[2048,768]{1,0:T(8,128)}) fusion(bf16[2048,384]{1,0:T(8,128)(2,1)} %bitcast.23.got_ref, bf16[2048,384]{1,0:T(8,128)(2,1)S(1)} %bitcast.75, f32[768]{0:T(1024)S(1)} %maximum_select_fusion.4, bf16[2048,768]{1,0:T(8,128)(2,1)S(1)} %copy-done.6, bf16[768,768]{1,0:T(8,128)(2,1)S(1)} %maximum_select_fusion.q_ref), kind=kOutput, calls=%fused_computation.14 | convolution fusion | flops 2426929152 | bytes 16911360 | tf_op jit(solution)/shard_map/dot_general | solution.py:1208
  171.0 3.1 fusion.39
  175.0 1.8 copy-done.3
  176.8 2.6 add_convert_fusion.normed_ref
  179.4 106.1 %feed_forward.1 = (f32[2048,768]{1,0:T(8,128)}, f32[2048,768]{1,0:T(8,128)}, bf16[2,16,3,48,1536]{4,3,2,1,0:T(8,128)(2,1)}) custom-call(bf16[2048,768]{1,0:T(8,128)(2,1)} %add_convert_fusion.normed_ref, bf16[2048,768]{1,0:T(8,128)(2,1)} %broadcast_select_fusion.cot_ref, bf16[2,768,5376]{2,1,0:T(8,128)(2,1)} %bitcast.79, bf16[2,768,5376]{2,1,0:T(8,128)(2,1)} %bitcast.80, ...), custom_call_target="tpu_custom_call" | custom-call | flops 86973087744 | bytes 56623104 | tf_op jit(solution)/shard_map/feed_forward/pallas_call | solution.py:532
  285.6 26.8 %mixer_back.1 = (f32[2048,768]{1,0:T(8,128)}, bf16[2048,768]{1,0:T(8,128)(2,1)}, f32[2048,768]{1,0:T(8,128)}, bf16[2048,768]{1,0:T(8,128)(2,1)}, bf16[2048,384]{...) custom-call(s32[1]{0:T(128)} %bitcast.core_ref, ...), custom_call_target="tpu_custom_call" | custom-call | flops 7247757312 | bytes 62914560 | tf_op jit(solution)/shard_map/mixer_back/pallas_call | solution.py:647
  312.4 5.9 %collective-permute-start.4 = (bf16[2048,384]{1,0:T(8,128)(2,1)}, bf16[2048,384]{1,0:T(8,128)(2,1)S(1)}, u32[]{:S(2)}, u32[]{:S(2)}) collective-permute-start(bf16[2048,384]{1,0:T(8,128)(2,1)} %get-tuple-element.59), channel_id=1, source_target_pairs={{0,2},{1,3},{2,0},{3,1},{4,6},{5,7},{6,4},{7,5},{8,10},{9,11},{10,... | collective-permute-start | bytes 4718600 | tf_op jit(solution)/shard_map/ppermute | solution.py:1095
  318.2 2.3 collective-permute-start.3
  322.7 44.9 %conv_backward.1 = (bf16[2,2048,384]{2,1,0:T(8,128)(2,1)}, bf16[2,2048,384]{2,1,0:T(8,128)(2,1)}, f32[3,384]{1,0:T(4,128)}, f32[3,384]{1,0:T(4,128)}) custom-call(s32[7]{0:T(128)} %pad_add_fusion.meta, bf16[16,128,384]{2,1,0:T(8,128)(2,1)} %bitcast.76, bf16[16,128,384]{2,1,0:T(8,128)(2,1)} %bitcast.77, ...), custom_call_target="tpu_custom_call" | custom-call | flops 1572864 | bytes 1572864 | tf_op jit(solution)/shard_map/conv_backward/pallas_call | solution.py:399
  370.8 7.4 %convert_select_fusion.1 = f32[2048,768]{1,0:T(8,128)} fusion(f32[2048,768]{1,0:T(8,128)} %get-tuple-element.55, bf16[2048,768]{1,0:T(8,128)(2,1)} %collective-permute-done.3, pred[]{:T(512)S(6)} %eq.4), kind=kLoop, calls=%fused_computation.11 | loop fusion | flops 3145728 | bytes 15728641 | tf_op jit(solution)/shard_map/jit(_where)/select_n | solution.py:1107
  378.2 1.8 copy-done.13
  380.0 21.5 %entry_back.1 = (f32[2048,768]{1,0:T(8,128)}, bf16[2048,768]{1,0:T(8,128)(2,1)}, bf16[768,1536]{1,0:T(8,128)(2,1)}, f32[8,768]{1,0:T(8,128)}) custom-call(s32[1]{0:T(128)} %bitcast.core_ref, bf16[2048,768]{1,0:T(8,128)(2,1)} %get-tuple-element.57.d_q_ref, bf16[2,2048,384]{2,1,0:T(8,128)(2,1)} %get-tuple-element.63.own_ref, bf16[2,2048,384]{2,1,0:T(8,128)(2,1)} %copy-done.13, ...), custom_call_target="tpu_custom_call" | custom-call | bytes 1572864 | tf_op jit(solution)/shard_map/entry_back/pallas_call | solution.py:734
  403.2 1.9 copy-done
  405.1 1.7 copy-done.1
  406.8 1.7 copy-done.2
  408.5 67.9 %closing.1 = (bf16[2048,768]{1,0:T(8,128)(2,1)S(1)}, f32[24,1664]{1,0:T(8,128)S(1)}, f32[24,1536]{1,0:T(8,128)S(1)}) custom-call(bf16[2048,768]{1,0:T(8,128)(2,1)S(1)} %copy-done, bf16[4,2,2,2,24,1536]{5,4,3,2,1,0:T(8,128)(2,1)S(1)} %bitcast.59, bf16[4,2,2,2,24,128]{5,4,3,2,1,0:T(8,128)(2,1)S(1)} %bitcast.61, bf16[4,2,2,2,24,1536]{5,4,3,2,1,0:T(8,128)(2,1)S(1)} %bitcast.60), custom_call_target="tpu_custom_call" | custom-call | tf_op jit(solution)/shard_map/closing/pallas_call | solution.py:1029
  480.5 6.1 %convert_select_fusion = f32[2048,768]{1,0:T(8,128)} fusion(f32[2048,768]{1,0:T(8,128)} %get-tuple-element.66, bf16[2048,768]{1,0:T(8,128)(2,1)S(1)} %get-tuple-element.74, pred[]{:T(512)S(6)} %eq.4), kind=kLoop, calls=%fused_computation.10 | loop fusion | flops 3145728 | bytes 15728641 | tf_op jit(solution)/shard_map/jit(_where)/select_n | solution.py:1375
  488.5 1.8 fusion.28
  (156 shorter events, 32.9 us)
Async XLA Ops:
  7.2 152.6 %all-gather.2.cloned.1.call-start = ((), (), s32[]{:S(2)}) async-start(), calls=%async_computation.1 | async-start | bytes 17031168 | tf_op jit(solution)/shard_map/all_gather | solution.py:1171
  10.6 476.0 %reduce-scatter.2.cloned.1.call-start = ((), (), s32[]{:S(2)}) async-start(), calls=%async_computation.2 | async-start | bytes 14598144 | tf_op jit(solution)/shard_map/reduce_scatter | solution.py:1264
  92.4 78.6 %copy-start.4 = (bf16[2048,768]{1,0:T(8,128)(2,1)}, bf16[2048,768]{1,0:T(8,128)(2,1)S(1)}, u32[]{:S(2)}) copy-start(bf16[2048,768]{1,0:T(8,128)(2,1)S(1)} %get-tuple-element.122.rows_ref) | copy-start | bytes 9437188
  92.4 2.4 copy-start.9
  92.5 3.1 copy-start.12
  96.3 2.0 copy-start.7
  96.4 2.0 copy-start.8
  98.4 5.7 %slice-start = ((s8[6291456]{0:T(1024)(128)(4,1)}), s8[4194304]{0:T(1024)(128)(4,1)S(1)}, s32[]{:S(2)}) async-start(s8[6291456]{0:T(1024)(128)(4,1)} %bitcast.62), calls=%async_computation.3 | async-start | bytes 8388608
  99.7 4.0 copy-start.5
  99.7 4.4 slice-start.1
  103.6 5.7 %copy-start.22 = (s32[16]{0:T(128)S(1)}, s32[16]{0:T(128)}, u32[]{:S(2)}) copy-start(s32[16]{0:T(128)} %param.23) | copy-start | bytes 196
  103.6 6.3 %copy-start.20 = (s32[1,4]{1,0:T(1,128)S(1)}, s32[1,4]{1,0:T(1,128)}, u32[]{:S(2)}) copy-start(s32[1,4]{1,0:T(1,128)} %lengths_ref.1) | copy-start | bytes 52
  103.7 6.3 %copy-start.21 = (s32[1,4]{1,0:T(1,128)S(1)}, s32[1,4]{1,0:T(1,128)}, u32[]{:S(2)}) copy-start(s32[1,4]{1,0:T(1,128)} %get-tuple-element.49) | copy-start | bytes 52
  103.7 14.9 %collective-permute-start = (bf16[2048,768]{1,0:T(8,128)(2,1)}, bf16[2048,768]{1,0:T(8,128)(2,1)}, u32[]{:S(2)}, u32[]{:S(2)}) collective-permute-start(bf16[2048,768]{1,0:T(8,128)(2,1)} %add_convert_fusion.1), channel_id=1, source_target_pairs={{0,2},{1,3},{2,0},{3,1},{4,6},{5,7},{6,4},{7,5},{8,10},{9,11},{10,... | collective-permute-start | bytes 9437192 | tf_op jit(solution)/shard_map/ppermute | solution.py:1095
  106.1 48.9 %collective-permute-start.2 = (bf16[2048,768]{1,0:T(8,128)(2,1)}, bf16[2048,768]{1,0:T(8,128)(2,1)}, u32[]{:S(2)}, u32[]{:S(2)}) collective-permute-start(bf16[2048,768]{1,0:T(8,128)(2,1)} %convert_element_type.53), channel_id=1, source_target_pairs={{1,2},{2,1},{5,6},{6,5},{9,10},{10,9},{13,14},{14,13},{17,18},{18,... | collective-permute-start | bytes 9437192 | tf_op jit(solution)/shard_map/ppermute | solution.py:1095
  154.9 8.2 %collective-permute-start.1 = (bf16[16,128,384]{2,1,0:T(8,128)(2,1)}, bf16[16,128,384]{2,1,0:T(8,128)(2,1)}, u32[]{:S(2)}, u32[]{:S(2)}) collective-permute-start(bf16[16,128,384]{2,1,0:T(8,128)(2,1)} %get-tuple-element.52), channel_id=1, source_target_pairs={{0,2},{1,3},{2,0},{3,1},{4,6},{5,7},{6,4},{7,5},{8,10},{9,11},{10,... | collective-permute-start | bytes 4718600 | tf_op jit(solution)/shard_map/ppermute | solution.py:1095
  162.2 2.7 copy-start.6
  162.2 3.2 copy-start.15
  162.6 8.4 %copy-start.10 = (bf16[768,768]{1,0:T(8,128)(2,1)}, bf16[768,768]{1,0:T(8,128)(2,1)S(1)}, u32[]{:S(2)}) copy-start(bf16[768,768]{1,0:T(8,128)(2,1)S(1)} %maximum_select_fusion.q_ref) | copy-start | bytes 3538948
  163.0 8.0 %copy-start.11 = (bf16[768,768]{1,0:T(8,128)(2,1)}, bf16[768,768]{1,0:T(8,128)(2,1)S(1)}, u32[]{:S(2)}) copy-start(bf16[768,768]{1,0:T(8,128)(2,1)S(1)} %maximum_select_fusion.2.out_weight_ref) | copy-start | bytes 3538948
  171.0 3.1 copy-start.14
  174.1 2.7 copy-start.3
  312.4 9.1 %collective-permute-start.4 = (bf16[2048,384]{1,0:T(8,128)(2,1)}, bf16[2048,384]{1,0:T(8,128)(2,1)S(1)}, u32[]{:S(2)}, u32[]{:S(2)}) collective-permute-start(bf16[2048,384]{1,0:T(8,128)(2,1)} %get-tuple-element.59), channel_id=1, source_target_pairs={{0,2},{1,3},{2,0},{3,1},{4,6},{5,7},{6,4},{7,5},{8,10},{9,11},{10,... | collective-permute-start | bytes 4718600 | tf_op jit(solution)/shard_map/ppermute | solution.py:1095
  318.2 52.5 %collective-permute-start.3 = (bf16[2048,768]{1,0:T(8,128)(2,1)}, bf16[2048,768]{1,0:T(8,128)(2,1)}, u32[]{:S(2)}, u32[]{:S(2)}) collective-permute-start(bf16[2048,768]{1,0:T(8,128)(2,1)} %get-tuple-element.56), channel_id=1, source_target_pairs={{1,2},{2,1},{5,6},{6,5},{9,10},{10,9},{13,14},{14,13},{17,18},{18,... | collective-permute-start | bytes 9437192 | tf_op jit(solution)/shard_map/ppermute | solution.py:1095
  322.7 46.0 %copy-start.23 = (s32[16]{0:T(128)S(1)}, s32[16]{0:T(128)}, u32[]{:S(2)}) copy-start(s32[16]{0:T(128)} %param.23) | copy-start | bytes 196
  322.7 47.3 %copy-start.17 = (f32[32,384]{1,0:T(8,128)S(1)}, f32[32,384]{1,0:T(8,128)}, u32[]{:S(2)}) copy-start(f32[32,384]{1,0:T(8,128)} %get-tuple-element.62.refs_8_) | copy-start | bytes 147460
  322.7 47.3 %copy-start.18 = (f32[8,768]{1,0:T(8,128)S(1)}, f32[8,768]{1,0:T(8,128)}, u32[]{:S(2)}) copy-start(f32[8,768]{1,0:T(8,128)} %get-tuple-element.70) | copy-start | bytes 73732
  367.6 10.7 %collective-permute-start.5 = (bf16[2,2048,384]{2,1,0:T(8,128)(2,1)}, bf16[2,2048,384]{2,1,0:T(8,128)(2,1)S(1)}, u32[]{:S(2)}, u32[]{:S(2)}) collective-permute-start(bf16[2,2048,384]{2,1,0:T(8,128)(2,1)} %get-tuple-element.64), channel_id=1, source_target_pairs={{0,2},{1,3},{2,0},{3,1},{4,6},{5,7},{6,4},{7,5},{8,10},{9,11},{10,... | collective-permute-start | bytes 9437192 | tf_op jit(solution)/shard_map/ppermute | solution.py:1095
  370.0 8.2 %copy-start.19 = (bf16[8,768]{1,0:T(8,128)(2,1)}, bf16[8,768]{1,0:T(8,128)(2,1)S(1)}, u32[]{:S(2)}) copy-start(bf16[8,768]{1,0:T(8,128)(2,1)S(1)} %convert.23) | copy-start | bytes 36868
  378.2 1.8 copy-start.13
  380.0 22.8 %slice-start.2 = ((bf16[8,768]{1,0:T(8,128)(2,1)}), bf16[2,768]{1,0:T(2,128)(2,1)S(1)}, s32[]{:S(2)}) async-start(bf16[8,768]{1,0:T(8,128)(2,1)} %copy-done.19), calls=%async_computation.5 | async-start | bytes 6144 | tf_op jit(solution)/shard_map/slice | solution.py:1287
  403.2 1.9 copy-start
  (3 other events, 4.5 us)
Sparse Core Ops, SparseCore 0:
  10.9 143.9 all-gather.1
  285.7 199.6 reduce-scatter.1
